TPU v7x, 32 devices: a whole 2x2x4 slice. The times are simulated.
32 devices in a mesh: clus: 8 (over z, x), src: 4 (over y, core).
Axes of the slice: x: 2, y: 2, z: 4, core: 2. Of those that a mesh axis runs over, the one named last changes fastest.
Arguments:
- embeddings: float32 [4096, 768], P(('clus', 'src'))
- cluster: int32 [4096], P(('clus', 'src')), may hold values from 0 to 63, as said below
Outputs:
- centroids: float32 [64, 768], P('clus')
- nearest: float32 [4096], P(('clus', 'src'))
Inputs may be any that keep to these rules, and one draw needn't show every extreme that they name: Of one device's 128 rows, at most 32 have clusters of one owner (cluster // 8); one owner receives exactly 32 rows from every device.
All inputs are finite; a program needn't handle non-finite values.
Results may differ from a plain program's by a relative error of at most 0.00032.
Values may be sent and summed in bfloat16 or wider, within the bound.
A program may use at most 64 MiB of HBM per device.

v0:
```python
import jax
import jax.numpy as jnp
from jax import lax
from jax.sharding import PartitionSpec as P

CLUS_DEV = 8


def block_maxima(current, own_unit, own_labels, own_global, other_unit, other_labels, other_global):
    scores = lax.dot_general(
        own_unit, other_unit, (((1,), (1,)), ((), ())), preferred_element_type=jnp.float32
    )
    allowed = (
        (own_labels[:, None] == other_labels[None, :])
        & (own_global[:, None] != other_global[None, :])
        & (own_labels[:, None] >= 0)
    )
    return jnp.maximum(current, jnp.max(jnp.where(allowed, scores, jnp.float32(-1.0)), axis=1))


def unit_rows(values):
    return (values * lax.rsqrt(jnp.sum(values * values, axis=1, keepdims=True) + 1e-06)).astype(
        jnp.bfloat16
    )


def normalized(owned):
    return owned * lax.rsqrt(jnp.sum(owned * owned, axis=1, keepdims=True) + 1e-06)


def on_device(embeddings, cluster):
    row_count = embeddings.shape[0]
    feature_dim = embeddings.shape[1]
    clus_count = lax.axis_size("clus")
    source_count = lax.axis_size("src")
    capacity = max(2, 2 * row_count // clus_count)
    slot_total = clus_count * capacity
    owner = cluster // CLUS_DEV
    member_hits = (owner[:, None] == jnp.arange(clus_count, dtype=jnp.int32)[None, :]).astype(
        jnp.int32
    )
    running = jnp.cumsum(member_hits, axis=0)
    position = jnp.sum(member_hits * running, axis=1) - 1
    slot_index = owner * capacity + position
    device_number = lax.axis_index("clus") * source_count + lax.axis_index("src")
    global_row = device_number * row_count + jnp.arange(row_count, dtype=jnp.int32)
    send_labels = jnp.full((slot_total,), -1, jnp.int32).at[slot_index].set(cluster)
    send_global = jnp.full((slot_total,), -1, jnp.int32).at[slot_index].set(global_row)
    count = lax.axis_size("clus") * CLUS_DEV
    inside = (cluster >= 0) & (cluster < count)
    segment = jnp.where(inside, cluster, count)
    owned = lax.psum_scatter(
        jax.ops.segment_sum(embeddings, segment, num_segments=count + 1)[:count],
        "clus",
        scatter_dimension=0,
        tiled=True,
    )
    owned = lax.psum(owned, "src")
    centroids = normalized(owned)
    unit = unit_rows(embeddings)
    send_unit = jnp.zeros((slot_total, feature_dim), jnp.bfloat16).at[slot_index].set(unit)
    received, recv_labels, recv_global = (
        lax.all_to_all(send_unit, "clus", split_axis=0, concat_axis=0, tiled=True),
        lax.all_to_all(send_labels, "clus", split_axis=0, concat_axis=0, tiled=True),
        lax.all_to_all(send_global, "clus", split_axis=0, concat_axis=0, tiled=True),
    )
    initial = jnp.full((slot_total,), -1.0, jnp.float32)
    piece_unit = lax.all_gather(received, "src", axis=0, tiled=True)
    piece_labels = lax.all_gather(recv_labels, "src", axis=0, tiled=True)
    piece_global = lax.all_gather(recv_global, "src", axis=0, tiled=True)
    length = piece_unit.shape[0]
    stacked = (
        piece_unit.reshape(length // slot_total, slot_total, feature_dim),
        piece_labels.reshape(length // slot_total, slot_total),
        piece_global.reshape(length // slot_total, slot_total),
    )

    def stepper(carried, sliced):
        return (
            block_maxima(
                carried, received, recv_labels, recv_global, sliced[0], sliced[1], sliced[2]
            ),
            None,
        )

    result, unused = lax.scan(stepper, initial, stacked)
    returned = lax.all_to_all(result, "clus", split_axis=0, concat_axis=0, tiled=True)
    nearest = returned[slot_index]
    return (centroids, nearest)


def solution(mesh):
    placed = (P(("clus", "src"), None), P(("clus", "src")))
    return jax.shard_map(
        on_device,
        mesh=mesh,
        in_specs=placed,
        out_specs=(P("clus", None), P(("clus", "src"))),
        check_vma=False,
    )
```

profile of v0, /device:TPU:0, one launch (start us, length us, event | category | flops | bytes accessed | tf_op | source)
XLA Modules:
  0.0 124.8 jit_solution(17371421840600976042)
XLA Ops:
  8.0 0.7 and_select_fusion
  9.1 1.1 multiply_reduce_fusion
  10.2 2.4 %scatter_custom_fusion.3 = bf16[256,768]{1,0:T(8,128)(2,1)} fusion(s32[128]{0:T(128)S(1)} %compare_select_fusion, f32[128,768]{1,0:T(8,128)} %param.4, f32[128]{0:T(128)S(1)} %add_rsqrt_fusion, bf16[]{:T(256)} %constant.32.clone.1), kind=kCustom, calls=%fused_computation.17 | custom fusion | flops 196608 | bytes 786946 | tf_op jit(solution)/shard_map/scatter | solution.py:61
  12.6 7.3 %all-to-all-start.2 = ((bf16[8,32,768]{2,1,0:T(8,128)(2,1)}), bf16[8,32,768]{2,1,0:T(8,128)(2,1)S(1)}, u32[]{:S(2)}, u32[]{:S(2)}) async-start(bf16[8,32,768]{2,1,0:T(8,128)(2,1)} %bitcast), calls=%async_computation.3 | async-start | bytes 786432 | tf_op jit(solution)/shard_map/all_to_all | solution.py:63
  19.9 1.9 %scatter_custom_fusion = f32[65,768]{1,0:T(8,128)S(1)} fusion(s32[128]{0:T(128)S(1)} %get-tuple-element.91, f32[128,768]{1,0:T(8,128)} %param.4, f32[]{:T(128)} %constant.27.clone.1), kind=kCustom, calls=%fused_computation.20 | custom fusion | flops 98304 | bytes 200192 | tf_op jit(solution)/shard_map/scatter-add | solution.py:53
  21.9 0.7 slice.6
  22.6 9.0 %all-to-all-done.2 = bf16[8,32,768]{2,1,0:T(8,128)(2,1)S(1)} async-done(((bf16[8,32,768]{2,1,0:T(8,128)(2,1)}), bf16[8,32,768]{2,1,0:T(8,128)(2,1)S(1)}, u32[]{:S(2)}, u32[]{:S(2)}) %all-to-all-start.2) | async-done | bytes 393248 | tf_op jit(solution)/shard_map/all_to_all | solution.py:63
  31.6 0.7 copy-done
  32.4 1.0 scatter_custom_fusion.2
  33.3 0.7 all_to_all.35
  34.0 3.6 %all-to-all-start.1 = ((s32[8,32,1]{1,2,0:T(1,128)}), s32[8,32,1]{1,2,0:T(1,128)S(1)}, u32[]{:S(2)}, u32[]{:S(2)}) async-start(s32[8,32,1]{1,2,0:T(1,128)} %all_to_all.35), calls=%async_computation.2 | async-start | bytes 8192 | tf_op jit(solution)/shard_map/all_to_all | solution.py:65
  37.7 1.1 scatter_custom_fusion.1
  38.8 0.7 all_to_all.32
  39.5 4.7 %all-to-all-done.1 = s32[8,32,1]{1,2,0:T(1,128)S(1)} async-done(((s32[8,32,1]{1,2,0:T(1,128)}), s32[8,32,1]{1,2,0:T(1,128)S(1)}, u32[]{:S(2)}, u32[]{:S(2)}) %all-to-all-start.1) | async-done | bytes 1056 | tf_op jit(solution)/shard_map/all_to_all | solution.py:65
  44.1 3.3 %all-to-all-start = ((s32[8,32,1]{1,2,0:T(1,128)}), s32[8,32,1]{1,2,0:T(1,128)S(1)}, u32[]{:S(2)}, u32[]{:S(2)}) async-start(s32[8,32,1]{1,2,0:T(1,128)} %all_to_all.32), calls=%async_computation.1 | async-start | bytes 8192 | tf_op jit(solution)/shard_map/all_to_all | solution.py:64
  47.9 0.6 reduce.14
  48.7 5.1 %all-gather.1 = s32[4,1,256]{2,1,0:T(1,128)S(1)} all-gather(s32[1,1,256]{2,1,0:T(1,128)S(1)} %reshape.90), channel_id=1, replica_groups=mesh['clus'=8,'src'=4] {'src'}, dimensions={0}, use_global_device_ids=true | all-gather | bytes 5120 | tf_op jit(solution)/shard_map/all_gather | solution.py:70
  53.8 0.6 reduce.13
  54.5 5.1 %all-gather = s32[4,1,256]{2,1,0:T(1,128)S(1)} all-gather(s32[1,1,256]{2,1,0:T(1,128)S(1)} %reshape.88), channel_id=1, replica_groups=mesh['clus'=8,'src'=4] {'src'}, dimensions={0}, use_global_device_ids=true | all-gather | bytes 5120 | tf_op jit(solution)/shard_map/all_gather | solution.py:69
  59.5 27.0 %reduce-scatter.2.cloned.1.call-done = f32[8,768]{1,0:T(8,128)} async-done(((f32[64,768]{1,0:T(8,128)}), f32[8,768]{1,0:T(8,128)}) %reduce-scatter.2.cloned.1.call-update) | async-done | bytes 24592 | tf_op jit(solution)/shard_map/reduce_scatter | solution.py:52
  86.6 10.8 %psum.7 = f32[8,768]{1,0:T(8,128)S(1)} all-reduce(f32[8,768]{1,0:T(8,128)} %reduce-scatter.2.cloned.1.call-done), channel_id=1, replica_groups=mesh['clus'=8,'src'=4] {'src'}, use_global_device_ids=true, to_apply=%region_2.3 | all-reduce | flops 6144 | bytes 49152 | tf_op jit(solution)/shard_map/psum | solution.py:58
  97.5 6.0 %while.11 = (s32[]{:T(128)}, f32[256]{0:T(256)S(1)}, s32[256]{0:T(256)S(1)}, s32[4,256]{1,0:T(4,128)S(1)}, s32[256]{0:T(256)S(1)}, /*index=5*/s32[4,256]{1,0:T(4...) while((s32[]{:T(128)}, f32[256]{0:T(256)S(1)}, ...), condition=%wide.region_12.13_spmd.clone, body=%wide.region_10.12_spmd.clone.sunk | while | flops 101057024 | bytes 800883 | solution.py:86
  97.6 1.4 %fusion.21 = f32[256]{0:T(256)S(1)} fusion(bf16[256,768]{1,0:T(8,128)(2,1)} %get-tuple-element.172, bf16[4,256,768]{2,1,0:T(8,128)(2,1)} %get-tuple-element.171, s32[]{:T(128)} %get-tuple-element.155, s32[256]{0:T(256)S(1)} %get-tuple-element.169, s32[256]{0:T(256)S(1)} %get-tuple-element.167, s32[256]{0:T(256)S(1)} %bitcast.41, ...), kind=kOutput, calls=%fused_computation.7.clone.1 | convolution fusion | flops 101056256 | bytes 792320 | tf_op jit(solution)/shard_map/while/body/eval_jaxpr/dot_general | solution.py:10
  99.1 1.4 %fusion.21 = f32[256]{0:T(256)S(1)} fusion(bf16[256,768]{1,0:T(8,128)(2,1)} %get-tuple-element.172, bf16[4,256,768]{2,1,0:T(8,128)(2,1)} %get-tuple-element.171, s32[]{:T(128)} %get-tuple-element.155, s32[256]{0:T(256)S(1)} %get-tuple-element.169, s32[256]{0:T(256)S(1)} %get-tuple-element.167, s32[256]{0:T(256)S(1)} %bitcast.41, ...), kind=kOutput, calls=%fused_computation.7.clone.1 | convolution fusion | flops 101056256 | bytes 792320 | tf_op jit(solution)/shard_map/while/body/eval_jaxpr/dot_general | solution.py:10
  100.6 1.5 %fusion.21 = f32[256]{0:T(256)S(1)} fusion(bf16[256,768]{1,0:T(8,128)(2,1)} %get-tuple-element.172, bf16[4,256,768]{2,1,0:T(8,128)(2,1)} %get-tuple-element.171, s32[]{:T(128)} %get-tuple-element.155, s32[256]{0:T(256)S(1)} %get-tuple-element.169, s32[256]{0:T(256)S(1)} %get-tuple-element.167, s32[256]{0:T(256)S(1)} %bitcast.41, ...), kind=kOutput, calls=%fused_computation.7.clone.1 | convolution fusion | flops 101056256 | bytes 792320 | tf_op jit(solution)/shard_map/while/body/eval_jaxpr/dot_general | solution.py:10
  102.1 1.4 %fusion.21 = f32[256]{0:T(256)S(1)} fusion(bf16[256,768]{1,0:T(8,128)(2,1)} %get-tuple-element.172, bf16[4,256,768]{2,1,0:T(8,128)(2,1)} %get-tuple-element.171, s32[]{:T(128)} %get-tuple-element.155, s32[256]{0:T(256)S(1)} %get-tuple-element.169, s32[256]{0:T(256)S(1)} %get-tuple-element.167, s32[256]{0:T(256)S(1)} %bitcast.41, ...), kind=kOutput, calls=%fused_computation.7.clone.1 | convolution fusion | flops 101056256 | bytes 792320 | tf_op jit(solution)/shard_map/while/body/eval_jaxpr/dot_general | solution.py:10
  103.6 0.7 all_to_all.41
  104.2 3.6 %all-to-all-start.3 = ((f32[8,32,1]{1,2,0:T(1,128)}), f32[8,32,1]{1,2,0:T(1,128)S(1)}, u32[]{:S(2)}, u32[]{:S(2)}) async-start(f32[8,32,1]{1,2,0:T(1,128)} %bitcast.3), calls=%async_computation.4 | async-start | bytes 8192 | tf_op jit(solution)/shard_map/all_to_all | solution.py:87
  107.8 0.7 broadcast_multiply_fusion
  108.5 5.8 %all-to-all-done.3 = f32[8,32,1]{1,2,0:T(1,128)S(1)} async-done(((f32[8,32,1]{1,2,0:T(1,128)}), f32[8,32,1]{1,2,0:T(1,128)S(1)}, u32[]{:S(2)}, u32[]{:S(2)}) %all-to-all-start.3) | async-done | bytes 1056 | tf_op jit(solution)/shard_map/all_to_all | solution.py:87
  114.8 0.7 reduce.15
  115.6 1.8 %gather_fusion = f32[128]{0:T(128)} fusion(f32[256]{0:T(256)S(1)} %all_to_all.43, s32[1024]{0:T(1024)S(1)} %pad_clamp_fusion), kind=kCustom, calls=%fused_computation | custom fusion | bytes 1536 | tf_op jit(solution)/shard_map/gather | solution.py:88
  (38 shorter events, 2.3 us)
Async XLA Ops:
  12.6 18.9 %all-to-all-start.2 = ((bf16[8,32,768]{2,1,0:T(8,128)(2,1)}), bf16[8,32,768]{2,1,0:T(8,128)(2,1)S(1)}, u32[]{:S(2)}, u32[]{:S(2)}) async-start(bf16[8,32,768]{2,1,0:T(8,128)(2,1)} %bitcast), calls=%async_computation.3 | async-start | bytes 786432 | tf_op jit(solution)/shard_map/all_to_all | solution.py:63
  19.9 66.7 %reduce-scatter.2.cloned.1.call-start = ((), (), s32[]{:S(2)}) async-start(), calls=%async_computation.5 | async-start | bytes 221184 | tf_op jit(solution)/shard_map/reduce_scatter | solution.py:52
  22.6 74.9 %all-gather.4.cloned.1.call-start = ((), (), s32[]{:S(2)}) async-start(), calls=%async_computation.6 | async-start | bytes 1966080 | tf_op jit(solution)/shard_map/all_gather | solution.py:68
  31.6 0.7 copy-start
  34.0 10.1 %all-to-all-start.1 = ((s32[8,32,1]{1,2,0:T(1,128)}), s32[8,32,1]{1,2,0:T(1,128)S(1)}, u32[]{:S(2)}, u32[]{:S(2)}) async-start(s32[8,32,1]{1,2,0:T(1,128)} %all_to_all.35), calls=%async_computation.2 | async-start | bytes 8192 | tf_op jit(solution)/shard_map/all_to_all | solution.py:65
  44.1 9.6 %all-to-all-start = ((s32[8,32,1]{1,2,0:T(1,128)}), s32[8,32,1]{1,2,0:T(1,128)S(1)}, u32[]{:S(2)}, u32[]{:S(2)}) async-start(s32[8,32,1]{1,2,0:T(1,128)} %all_to_all.32), calls=%async_computation.1 | async-start | bytes 8192 | tf_op jit(solution)/shard_map/all_to_all | solution.py:64
  104.2 10.1 %all-to-all-start.3 = ((f32[8,32,1]{1,2,0:T(1,128)}), f32[8,32,1]{1,2,0:T(1,128)S(1)}, u32[]{:S(2)}, u32[]{:S(2)}) async-start(f32[8,32,1]{1,2,0:T(1,128)} %bitcast.3), calls=%async_computation.4 | async-start | bytes 8192 | tf_op jit(solution)/shard_map/all_to_all | solution.py:87
Sparse Core Ops, SparseCore 0:
  24.0 62.5 reduce-scatter.1
Sparse Core Ops, SparseCore 1:
  32.4 18.6 all-gather.3
where the time goes:
time: 125 us
  waiting for transfers between devices  46.5 us (37%)
  blocking collectives  20.9 us (17%)
  starting transfers between devices  17.9 us (14%)
  between operations  15.6 us (12%)
  other arithmetic  9.22 us (7%)
  local copies, waits for them, and re-layouts  8.74 us (7%)
  matrix products  5.79 us (5%)
    reduce_scatter x1, waiting for transfers between devices, on_device(): lax.psum_scatter(jax.ops.segment_sum(embeddings, segment, num_segments=co...  27 us
    psum x1, blocking collectives, on_device(): owned = lax.psum(owned, 'src')  10.8 us
    all_to_all x1, waiting for transfers between devices, on_device(): lax.all_to_all(send_unit, 'clus', split_axis=0, concat_axis=0, tiled=True)  8.97 us
    all_to_all x1, starting transfers between devices, on_device(): lax.all_to_all(send_unit, 'clus', split_axis=0, concat_axis=0, tiled=True)  7.25 us
    dot_general x4, matrix products, block_maxima(): lax.dot_general(own_unit, other_unit, (((1,), (1,)), ((), ())), preferred...  5.79 us
    all_to_all x1, waiting for transfers between devices, on_device(): lax.all_to_all(result, 'clus', split_axis=0, concat_axis=0, tiled=True)  5.79 us
    all_gather x1, blocking collectives, on_device(): piece_global = lax.all_gather(recv_global, 'src', axis=0, tiled=True)  5.06 us
    all_gather x1, blocking collectives, on_device(): piece_labels = lax.all_gather(recv_labels, 'src', axis=0, tiled=True)  5.06 us
  transfers between devices with their start and end apart: 6, of which 4 were waited for; matrix products, arithmetic and copies ran while one was open for 6% of the time, Pallas kernels for 0%

commit v1 on v0

--- a/solution.py
+++ b/solution.py
@@ -1,9 +1,322 @@
+import functools
+
 import jax
 import jax.numpy as jnp
 from jax import lax
+from jax.experimental import pallas as pl
+from jax.experimental.pallas import tpu as pltpu
 from jax.sharding import PartitionSpec as P
 
 CLUS_DEV = 8
+MESH = pl.DeviceIdType.MESH
+EPS = 1e-06
+
+
+def partner(index, distance, count):
+    total = 0
+    bit = 1
+    while bit < count:
+        value = (index // bit) % 2
+        total = total + bit * ((1 - value) if (distance // bit) % 2 else value)
+        bit *= 2
+    return total
+
+
+def exact_parts(values):
+    high = values.astype(jnp.bfloat16)
+    rest = values - high.astype(jnp.float32)
+    middle = rest.astype(jnp.bfloat16)
+    low = (rest - middle.astype(jnp.float32)).astype(jnp.bfloat16)
+    return high, middle, low
+
+
+def dot_t(left, right):
+    return lax.dot_general(left, right, (((1,), (1,)), ((), ())), preferred_element_type=jnp.float32)
+
+
+def own_lanes(rows_ref, n_clus, cap):
+    width = n_clus * cap
+    group = lax.broadcasted_iota(jnp.int32, (1, width), 1) // cap
+    total = jnp.zeros((1, width), jnp.float32)
+    for d in range(n_clus):
+        total = jnp.where(group == d, rows_ref[d], total)
+    return total
+
+
+def owner_kernel(
+    n_clus,
+    n_src,
+    cap,
+    cluster_ref,
+    emb_ref,
+    cent_ref,
+    near_ref,
+    packed,
+    gathered,
+    labels,
+    shard_labels,
+    partial,
+    partial_in,
+    owned,
+    owned_in,
+    cents,
+    maxima,
+    row_sem,
+    y_sem,
+    core_sem,
+    diag_sem,
+    label_sem,
+    shard_sem,
+    partial_sem,
+    owned_sem,
+    cent_sem,
+    max_sem,
+):
+    rows, depth = emb_ref.shape
+    slots = n_clus * cap
+    per = CLUS_DEV // n_src
+    me = lax.axis_index("clus")
+    src = lax.axis_index("src")
+    clus_peer = [partner(me, d, n_clus) for d in range(n_clus)]
+    src_peer = [partner(src, e, n_src) for e in range(n_src)]
+    at_clus = [(clus_peer[d], src) for d in range(n_clus)]
+    at_src = [(me, src_peer[e]) for e in range(n_src)]
+
+    def copy(source, target, sems, slot, device):
+        return pltpu.make_async_remote_copy(
+            src_ref=source,
+            dst_ref=target,
+            send_sem=sems.at[0, slot],
+            recv_sem=sems.at[1, slot],
+            device_id=device,
+            device_id_type=MESH,
+        )
+
+    barrier = pltpu.get_barrier_semaphore()
+    others = [at_clus[d] for d in range(1, n_clus)] + [at_src[e] for e in range(1, n_src)]
+    for device in others:
+        pl.semaphore_signal(barrier, inc=1, device_id=device, device_id_type=MESH)
+
+    cluster = cluster_ref[...]
+    within = cluster % CLUS_DEV
+    distance = jnp.bitwise_xor(cluster // CLUS_DEV, me)
+    hits = lax.broadcasted_iota(jnp.int32, (n_clus, rows), 0) == distance
+    earlier = lax.broadcasted_iota(jnp.int32, (rows, rows), 0) < lax.broadcasted_iota(
+        jnp.int32, (rows, rows), 1
+    )
+    before = jnp.dot(
+        jnp.where(hits, 1.0, 0.0).astype(jnp.bfloat16),
+        jnp.where(earlier, 1.0, 0.0).astype(jnp.bfloat16),
+        preferred_element_type=jnp.float32,
+    )
+    place = jnp.sum(jnp.where(hits, before, 0.0), axis=0, keepdims=True).astype(jnp.int32)
+    slot = distance * cap + place
+    pick = jnp.where(lax.broadcasted_iota(jnp.int32, (slots, rows), 0) == slot, 1.0, 0.0).astype(
+        jnp.bfloat16
+    )
+
+    emb = emb_ref[...]
+    unit = (emb * lax.rsqrt(jnp.sum(emb * emb, axis=1, keepdims=True) + EPS)).astype(jnp.bfloat16)
+    packed[...] = (
+        jnp.dot(pick, unit, preferred_element_type=jnp.float32)
+        .astype(jnp.bfloat16)
+        .reshape(n_clus, cap, depth)
+    )
+    gathered[0, 0] = packed[0]
+    label_row = dot_t(
+        jnp.broadcast_to((within + 1).astype(jnp.float32), (8, rows)).astype(jnp.bfloat16), pick
+    )[:1]
+    labels[0] = label_row
+
+    label_copy = {
+        d: copy(labels.at[0], labels.at[d], label_sem, d, at_clus[d]) for d in range(1, n_clus)
+    }
+    row_copy = {
+        d: copy(packed.at[d], gathered.at[0, d], row_sem, d, at_clus[d]) for d in range(1, n_clus)
+    }
+    core_copy = {
+        d: copy(gathered.at[0, d], gathered.at[1, d], core_sem, d, at_src[1]) for d in range(n_clus)
+    }
+    y_copy = {
+        d: copy(gathered.at[0, d], gathered.at[2, d], y_sem, d, at_src[2]) for d in range(n_clus)
+    }
+    diag_copy = {
+        d: copy(gathered.at[2, d], gathered.at[3, d], diag_sem, d, at_src[1]) for d in range(n_clus)
+    }
+    partial_copy = {
+        e: copy(partial.at[e], partial_in.at[e], partial_sem, e, at_src[e]) for e in range(1, n_src)
+    }
+    owned_copy = {
+        d: copy(owned.at[d], owned_in.at[d], owned_sem, d, at_clus[d]) for d in range(1, n_clus)
+    }
+    cent_copy = {
+        e: copy(cents.at[0], cents.at[e], cent_sem, e, at_src[e]) for e in range(1, n_src)
+    }
+    shard_copy = {
+        e: copy(shard_labels.at[0], shard_labels.at[e], shard_sem, e, at_src[e])
+        for e in range(1, n_src)
+    }
+    max_copy = {
+        d: copy(maxima.at[0], maxima.at[d], max_sem, d, at_clus[d]) for d in range(1, n_clus)
+    }
+
+    pl.semaphore_wait(barrier, len(others))
+    far_first = sorted(range(1, n_clus), key=lambda d: -d)
+    near_first = sorted(range(1, n_clus))
+    y_copy[0].start()
+    for d in far_first:
+        row_copy[d].start()
+    core_copy[0].start()
+    for d in near_first:
+        label_copy[d].start()
+
+    order = (
+        jnp.bitwise_xor(within // per, src) * (n_clus * per) + distance * per + within % per
+    )
+    count = n_src * n_clus * per
+    members = jnp.where(
+        lax.broadcasted_iota(jnp.int32, (count, rows), 0) == order, 2.0, 0.0
+    ).astype(jnp.bfloat16)
+    sums = jnp.zeros((count, depth), jnp.float32)
+    for part in exact_parts(emb * 0.5):
+        sums = sums + jnp.dot(members, part, preferred_element_type=jnp.float32)
+    partial[...] = sums.reshape(n_src, n_clus * per, depth)
+    for e in range(1, n_src):
+        partial_copy[e].start()
+
+    for d in near_first:
+        label_copy[d].wait_recv()
+    own_labels = own_lanes(labels, n_clus, cap)
+    shard_labels[0] = own_labels
+    for e in range(1, n_src):
+        shard_copy[e].start()
+
+    def reduce_sums():
+        total = partial[0]
+        for e in range(1, n_src):
+            partial_copy[e].wait_recv()
+            total = total + partial_in[e]
+        for d in range(n_clus):
+            owned[d] = total[d * per : (d + 1) * per]
+        for d in range(1, n_clus):
+            owned_copy[d].start()
+
+    def finish_sums():
+        total = owned[0]
+        for d in range(1, n_clus):
+            owned_copy[d].wait_recv()
+            total = total + owned_in[d]
+        cents[0] = total * lax.rsqrt(jnp.sum(total * total, axis=1, keepdims=True) + EPS)
+        for e in range(1, n_src):
+            cent_copy[e].start()
+
+    def shard_maxima(e):
+        scores = dot_t(gathered[e].reshape(slots, depth), gathered[0].reshape(slots, depth))
+        other = jnp.transpose(jnp.broadcast_to(shard_labels[e], (128, slots)))
+        other = jnp.concatenate([other] * (slots // 128), axis=1)
+        allowed = other == own_labels
+        if e == 0:
+            allowed = allowed & (
+                lax.broadcasted_iota(jnp.int32, (slots, slots), 0)
+                != lax.broadcasted_iota(jnp.int32, (slots, slots), 1)
+            )
+        return jnp.max(jnp.where(allowed, scores, -1.0), axis=0, keepdims=True)
+
+    waiting = [0]
+    for step, d in enumerate(near_first):
+        row_copy[d].wait_recv()
+        y_copy[d].start()
+        core_copy[d].start()
+        waiting.append(d)
+        if step == 1:
+            reduce_sums()
+        if step >= 2:
+            first = waiting.pop(0)
+            y_copy[first].wait_recv()
+            diag_copy[first].start()
+    best = shard_maxima(0)
+    finish_sums()
+    for d in waiting:
+        y_copy[d].wait_recv()
+        diag_copy[d].start()
+    for e in range(1, n_src):
+        shard_copy[e].wait_recv()
+    best = jnp.maximum(best, shard_maxima(2))
+    for d in range(n_clus):
+        core_copy[d].wait_recv()
+    best = jnp.maximum(best, shard_maxima(1))
+    for d in range(n_clus):
+        diag_copy[d].wait_recv()
+    maxima[0] = jnp.maximum(best, shard_maxima(3))
+    for d in far_first:
+        max_copy[d].start()
+
+    for e in range(1, n_src):
+        cent_copy[e].wait_recv()
+    for shard in range(n_src):
+        cent_ref[shard * per : (shard + 1) * per, :] = cents[src_peer[shard]]
+    for d in near_first:
+        max_copy[d].wait_recv()
+    near = jnp.zeros((8, rows), jnp.float32)
+    for part in exact_parts(jnp.broadcast_to(own_lanes(maxima, n_clus, cap), (8, slots))):
+        near = near + jnp.dot(part, pick, preferred_element_type=jnp.float32)
+    near_ref[...] = near[:1]
+
+    for copies in (
+        label_copy,
+        row_copy,
+        core_copy,
+        y_copy,
+        diag_copy,
+        partial_copy,
+        shard_copy,
+        owned_copy,
+        cent_copy,
+        max_copy,
+    ):
+        for started in copies.values():
+            started.wait_send()
+
+
+def one_kernel(n_clus, n_src, embeddings, cluster):
+    rows, depth = embeddings.shape
+    cap = 2 * rows // n_clus
+    slots = n_clus * cap
+    per = CLUS_DEV // n_src
+    f32, bf16 = jnp.float32, jnp.bfloat16
+    vmem = pl.BlockSpec(memory_space=pltpu.VMEM)
+    centroids, nearest = pl.pallas_call(
+        functools.partial(owner_kernel, n_clus, n_src, cap),
+        out_shape=(
+            jax.ShapeDtypeStruct((CLUS_DEV, depth), f32),
+            jax.ShapeDtypeStruct((1, rows), f32),
+        ),
+        in_specs=[vmem, vmem],
+        out_specs=(vmem, vmem),
+        scratch_shapes=[
+            pltpu.VMEM((n_clus, cap, depth), bf16),
+            pltpu.VMEM((n_src, n_clus, cap, depth), bf16),
+            pltpu.VMEM((n_clus, 1, slots), f32),
+            pltpu.VMEM((n_src, 1, slots), f32),
+            pltpu.VMEM((n_src, n_clus * per, depth), f32),
+            pltpu.VMEM((n_src, n_clus * per, depth), f32),
+            pltpu.VMEM((n_clus, per, depth), f32),
+            pltpu.VMEM((n_clus, per, depth), f32),
+            pltpu.VMEM((n_src, per, depth), f32),
+            pltpu.VMEM((n_clus, 1, slots), f32),
+        ]
+        + [
+            pltpu.SemaphoreType.DMA((2, count))
+            for count in (n_clus, n_clus, n_clus, n_clus, n_clus, n_src, n_src, n_clus, n_src, n_clus)
+        ],
+        compiler_params=pltpu.CompilerParams(
+            collective_id=0, has_side_effects=True, vmem_limit_bytes=32 * 1024 * 1024
+        ),
+        cost_estimate=pl.CostEstimate(
+            flops=2 * slots * slots * n_src * depth, bytes_accessed=rows * depth * 4, transcendentals=0
+        ),
+    )(cluster.reshape(1, rows), embeddings)
+    return centroids, nearest.reshape(rows)
 
 
 def block_maxima(current, own_unit, own_labels, own_global, other_unit, other_labels, other_global):
@@ -89,10 +402,28 @@
     return (centroids, nearest)
 
 
+def fits_one_kernel(n_clus, n_src, rows):
+    cap = 2 * rows // n_clus
+    return (
+        n_src == 4
+        and n_clus & (n_clus - 1) == 0
+        and cap % 16 == 0
+        and n_clus * cap % 128 == 0
+        and rows % 128 == 0
+    )
+
+
 def solution(mesh):
+    n_clus, n_src = mesh.shape["clus"], mesh.shape["src"]
+
+    def body(embeddings, cluster):
+        if fits_one_kernel(n_clus, n_src, embeddings.shape[0]):
+            return one_kernel(n_clus, n_src, embeddings, cluster)
+        return on_device(embeddings, cluster)
+
     placed = (P(("clus", "src"), None), P(("clus", "src")))
     return jax.shard_map(
-        on_device,
+        body,
         mesh=mesh,
         in_specs=placed,
         out_specs=(P("clus", None), P(("clus", "src"))),

time: 125 us -> 35.6 us (0.28)
  waiting for transfers between devices: 46.5 us -> 0 us
  Pallas kernels: 0 us -> 32 us
  blocking collectives: 20.9 us -> 0 us
  starting transfers between devices: 17.9 us -> 0 us
  between operations: 15.6 us -> 0.65 us
  other arithmetic: 9.22 us -> 0 us
  local copies, waits for them, and re-layouts: 8.74 us -> 2.77 us
  matrix products: 5.79 us -> 0 us
    pallas_call x0 -> x1, Pallas kernels: none -> 32 us  [one_kernel(): pl.pallas_call(functools.partial(owner_kernel, n_clus, n_src, cap), out_s...]
    reduce_scatter x1 -> x0, waiting for transfers between devices: 27 us -> none  [on_device(): lax.psum_scatter(jax.ops.segment_sum(embeddings, segment, num_segments=co...]
    all_to_all x4 -> x0, waiting for transfers between devices: 19.4 us -> none  [the longest x1 8.97 us: on_device(): lax.all_to_all(send_unit, 'clus', split_axis=0, concat_axis=0, tiled=True)]
    all_to_all x4 -> x0, starting transfers between devices: 17.8 us -> none  [the longest x1 7.25 us: on_device(): lax.all_to_all(send_unit, 'clus', split_axis=0, concat_axis=0, tiled=True)]
    psum x1 -> x0, blocking collectives: 10.8 us -> none  [on_device(): owned = lax.psum(owned, 'src')]
    all_gather x2 -> x0, blocking collectives: 10.1 us -> none  [the longest x1 5.06 us: on_device(): piece_global = lax.all_gather(recv_global, 'src', axis=0, tiled=True)]
    dot_general x4 -> x0, matrix products: 5.79 us -> none  [block_maxima(): lax.dot_general(own_unit, other_unit, (((1,), (1,)), ((), ())), preferred...]
    all_to_all x8 -> x0, local copies, waits for them, and re-layouts: 3.28 us -> none  [the longest x3 1.26 us: on_device(): lax.all_to_all(send_labels, 'clus', split_axis=0, concat_axis=0, tiled=True)]
  transfers between devices with their start and end apart: 6 -> 0, of which waited for: 4 -> 0; matrix products, arithmetic and copies ran while one was open for 6% -> 0% of each run, Pallas kernels for 0% -> 0%
where the time goes in v1:
time: 35.6 us; the launch traced here: 35.5 us
  Pallas kernels  32 us (90%)
  local copies, waits for them, and re-layouts  2.77 us (8%)
  between operations  0.65 us (2%)
    pallas_call x1, Pallas kernels, one_kernel(): pl.pallas_call(functools.partial(owner_kernel, n_clus, n_src, cap), out_s...  32 us
    unnamed x6, local copies, waits for them, and re-layouts  2.77 us

profile of v1, /device:TPU:0, one launch (start us, length us, event | category | flops | bytes accessed | tf_op | source)
XLA Modules:
  0.0 35.5 jit_solution(10536058829796860292)
XLA Ops:
  0.6 0.0 copy-start.1
  0.6 0.6 %copy-done.1 = s32[128]{0:T(128)S(1)} copy-done((s32[128]{0:T(128)S(1)}, s32[128]{0:T(128)}, u32[]{:S(2)}) %copy-start.1) | copy-done | bytes 536
  1.3 0.0 copy-start
  1.3 1.0 %copy-done = f32[128,768]{1,0:T(8,128)S(1)} copy-done((f32[128,768]{1,0:T(8,128)S(1)}, f32[128,768]{1,0:T(8,128)}, u32[]{:S(2)}) %copy-start) | copy-done | bytes 393240
  2.3 32.0 %shard_map.41 = (f32[8,768]{1,0:T(8,128)S(1)}, f32[1,128]{1,0:T(1,128)S(1)}) custom-call(s32[1,128]{1,0:T(1,128)S(1)} %bitcast.2, f32[128,768]{1,0:T(8,128)S(1)} %copy-done), custom_call_target="tpu_custom_call" | custom-call | flops 402653184 | bytes 393216 | tf_op jit(solution)/shard_map/pallas_call | solution.py:288
  34.3 0.6 %copy.6 = f32[8,768]{1,0:T(8,128)} copy(f32[8,768]{1,0:T(8,128)S(1)} %get-tuple-element.8) | data formatting | bytes 49152
  34.9 0.5 %copy.7 = f32[128]{0:T(128)} copy(f32[128]{0:T(128)S(1)} %bitcast.3) | data formatting | bytes 1024
Async XLA Ops:
  0.6 0.7 %copy-start.1 = (s32[128]{0:T(128)S(1)}, s32[128]{0:T(128)}, u32[]{:S(2)}) copy-start(s32[128]{0:T(128)} %param.3) | copy-start | bytes 1540
  1.3 1.0 %copy-start = (f32[128,768]{1,0:T(8,128)S(1)}, f32[128,768]{1,0:T(8,128)}, u32[]{:S(2)}) copy-start(f32[128,768]{1,0:T(8,128)} %emb_ref.1) | copy-start | bytes 1179652

commit v2 on v1

--- a/solution.py
+++ b/solution.py
@@ -47,10 +47,12 @@
     n_clus,
     n_src,
     cap,
+    cluster_hbm,
+    emb_hbm,
+    cent_ref,
+    near_ref,
     cluster_ref,
     emb_ref,
-    cent_ref,
-    near_ref,
     packed,
     gathered,
     labels,
@@ -71,6 +73,7 @@
     owned_sem,
     cent_sem,
     max_sem,
+    load_sem,
 ):
     rows, depth = emb_ref.shape
     slots = n_clus * cap
@@ -92,11 +95,16 @@
             device_id_type=MESH,
         )
 
+    load_cluster = pltpu.make_async_copy(cluster_hbm, cluster_ref, load_sem.at[0])
+    load_rows = pltpu.make_async_copy(emb_hbm, emb_ref, load_sem.at[1])
+    load_cluster.start()
+    load_rows.start()
     barrier = pltpu.get_barrier_semaphore()
     others = [at_clus[d] for d in range(1, n_clus)] + [at_src[e] for e in range(1, n_src)]
     for device in others:
         pl.semaphore_signal(barrier, inc=1, device_id=device, device_id_type=MESH)
 
+    load_cluster.wait()
     cluster = cluster_ref[...]
     within = cluster % CLUS_DEV
     distance = jnp.bitwise_xor(cluster // CLUS_DEV, me)
@@ -115,6 +123,7 @@
         jnp.bfloat16
     )
 
+    load_rows.wait()
     emb = emb_ref[...]
     unit = (emb * lax.rsqrt(jnp.sum(emb * emb, axis=1, keepdims=True) + EPS)).astype(jnp.bfloat16)
     packed[...] = (
@@ -161,14 +170,14 @@
     }
 
     pl.semaphore_wait(barrier, len(others))
-    far_first = sorted(range(1, n_clus), key=lambda d: -d)
-    near_first = sorted(range(1, n_clus))
+    half = n_clus // 2
+    turns = [d for near in range(half) for d in (half + near, near + 1)][: n_clus - 1]
+    for d in turns:
+        label_copy[d].start()
     y_copy[0].start()
-    for d in far_first:
+    for d in turns:
         row_copy[d].start()
     core_copy[0].start()
-    for d in near_first:
-        label_copy[d].start()
 
     order = (
         jnp.bitwise_xor(within // per, src) * (n_clus * per) + distance * per + within % per
@@ -184,12 +193,14 @@
     for e in range(1, n_src):
         partial_copy[e].start()
 
-    for d in near_first:
-        label_copy[d].wait_recv()
-    own_labels = own_lanes(labels, n_clus, cap)
-    shard_labels[0] = own_labels
-    for e in range(1, n_src):
-        shard_copy[e].start()
+    def send_labels():
+        for d in turns:
+            label_copy[d].wait_recv()
+        own_labels = own_lanes(labels, n_clus, cap)
+        shard_labels[0] = own_labels
+        for e in range(1, n_src):
+            shard_copy[e].start()
+        return own_labels
 
     def reduce_sums():
         total = partial[0]
@@ -222,40 +233,44 @@
             )
         return jnp.max(jnp.where(allowed, scores, -1.0), axis=0, keepdims=True)
 
+    def pass_on(d):
+        y_copy[d].wait_recv()
+        diag_copy[d].start()
+
     waiting = [0]
-    for step, d in enumerate(near_first):
+    for step, d in enumerate(turns):
         row_copy[d].wait_recv()
         y_copy[d].start()
         core_copy[d].start()
         waiting.append(d)
         if step == 1:
+            own_labels = send_labels()
+        if step == 2:
             reduce_sums()
         if step >= 2:
-            first = waiting.pop(0)
-            y_copy[first].wait_recv()
-            diag_copy[first].start()
+            pass_on(waiting.pop(0))
+    pass_on(waiting.pop(0))
     best = shard_maxima(0)
-    finish_sums()
-    for d in waiting:
-        y_copy[d].wait_recv()
-        diag_copy[d].start()
     for e in range(1, n_src):
         shard_copy[e].wait_recv()
-    best = jnp.maximum(best, shard_maxima(2))
     for d in range(n_clus):
         core_copy[d].wait_recv()
     best = jnp.maximum(best, shard_maxima(1))
+    for d in waiting:
+        pass_on(d)
+    finish_sums()
+    best = jnp.maximum(best, shard_maxima(2))
     for d in range(n_clus):
         diag_copy[d].wait_recv()
     maxima[0] = jnp.maximum(best, shard_maxima(3))
-    for d in far_first:
+    for d in turns:
         max_copy[d].start()
 
     for e in range(1, n_src):
         cent_copy[e].wait_recv()
     for shard in range(n_src):
         cent_ref[shard * per : (shard + 1) * per, :] = cents[src_peer[shard]]
-    for d in near_first:
+    for d in turns:
         max_copy[d].wait_recv()
     near = jnp.zeros((8, rows), jnp.float32)
     for part in exact_parts(jnp.broadcast_to(own_lanes(maxima, n_clus, cap), (8, slots))):
@@ -285,15 +300,18 @@
     per = CLUS_DEV // n_src
     f32, bf16 = jnp.float32, jnp.bfloat16
     vmem = pl.BlockSpec(memory_space=pltpu.VMEM)
+    hbm = pl.BlockSpec(memory_space=pltpu.HBM)
     centroids, nearest = pl.pallas_call(
         functools.partial(owner_kernel, n_clus, n_src, cap),
         out_shape=(
             jax.ShapeDtypeStruct((CLUS_DEV, depth), f32),
             jax.ShapeDtypeStruct((1, rows), f32),
         ),
-        in_specs=[vmem, vmem],
+        in_specs=[hbm, hbm],
         out_specs=(vmem, vmem),
         scratch_shapes=[
+            pltpu.VMEM((1, rows), jnp.int32),
+            pltpu.VMEM((rows, depth), f32),
             pltpu.VMEM((n_clus, cap, depth), bf16),
             pltpu.VMEM((n_src, n_clus, cap, depth), bf16),
             pltpu.VMEM((n_clus, 1, slots), f32),
@@ -308,9 +326,10 @@
         + [
             pltpu.SemaphoreType.DMA((2, count))
             for count in (n_clus, n_clus, n_clus, n_clus, n_clus, n_src, n_src, n_clus, n_src, n_clus)
-        ],
+        ]
+        + [pltpu.SemaphoreType.DMA((2,))],
         compiler_params=pltpu.CompilerParams(
-            collective_id=0, has_side_effects=True, vmem_limit_bytes=32 * 1024 * 1024
+            collective_id=0, has_side_effects=True, vmem_limit_bytes=56 * 1024 * 1024
         ),
         cost_estimate=pl.CostEstimate(
             flops=2 * slots * slots * n_src * depth, bytes_accessed=rows * depth * 4, transcendentals=0

time: 35.6 us -> 30.9 us (0.87)
  Pallas kernels: 32 us -> 28.2 us
  local copies, waits for them, and re-layouts: 2.77 us -> 1.86 us
    pallas_call x1, Pallas kernels: 32 us -> 28.2 us  [one_kernel(): pl.pallas_call(functools.partial(owner_kernel, n_clus, n_src, cap), out_s...]
    unnamed x6 -> x4, local copies, waits for them, and re-layouts: 2.77 us -> 1.86 us
where the time goes in v2:
time: 30.9 us; the launch traced here: 30.7 us
  Pallas kernels  28.2 us (91%)
  local copies, waits for them, and re-layouts  1.86 us (6%)
  between operations  0.65 us (2%)
    pallas_call x1, Pallas kernels, one_kernel(): pl.pallas_call(functools.partial(owner_kernel, n_clus, n_src, cap), out_s...  28.2 us
    unnamed x4, local copies, waits for them, and re-layouts  1.86 us

profile of v2, /device:TPU:0, one launch (start us, length us, event | category | flops | bytes accessed | tf_op | source)
XLA Modules:
  0.0 30.7 jit_solution(4376362702069643187)
XLA Ops:
  0.6 28.2 %shard_map.41 = (f32[8,768]{1,0:T(8,128)}, f32[1,128]{1,0:T(1,128)}) custom-call(s32[1,128]{1,0:T(1,128)} %bitcast.2, f32[128,768]{1,0:T(8,128)} %emb_hbm.1), custom_call_target="tpu_custom_call" | custom-call | flops 402653184 | bytes 393216 | tf_op jit(solution)/shard_map/pallas_call | solution.py:304
  28.8 0.0 copy-start
  28.8 1.3 %copy.6 = f32[8,768]{1,0:T(8,128)} copy(f32[8,768]{1,0:T(8,128)} %get-tuple-element.8) | data formatting | bytes 49152
  30.2 0.0 copy-done
  30.2 0.5 %copy.7 = f32[128]{0:T(128)} copy(f32[128]{0:T(128)S(1)} %bitcast.3) | data formatting | bytes 1024
Async XLA Ops:
  28.8 1.4 %copy-start = (f32[1,128]{1,0:T(1,128)S(1)}, f32[1,128]{1,0:T(1,128)}, u32[]{:S(2)}) copy-start(f32[1,128]{1,0:T(1,128)} %get-tuple-element.5) | copy-start | bytes 1540

commit v3 on v2

--- a/solution.py
+++ b/solution.py
@@ -153,7 +153,9 @@
         d: copy(gathered.at[2, d], gathered.at[3, d], diag_sem, d, at_src[1]) for d in range(n_clus)
     }
     partial_copy = {
-        e: copy(partial.at[e], partial_in.at[e], partial_sem, e, at_src[e]) for e in range(1, n_src)
+        0: copy(partial.at[1], partial_in.at[0], partial_sem, 0, at_src[1]),
+        1: copy(partial.at[3], partial_in.at[1], partial_sem, 1, at_src[1]),
+        2: copy(partial.at[2], partial_in.at[2], partial_sem, 2, at_src[2]),
     }
     owned_copy = {
         d: copy(owned.at[d], owned_in.at[d], owned_sem, d, at_clus[d]) for d in range(1, n_clus)
@@ -171,11 +173,13 @@
 
     pl.semaphore_wait(barrier, len(others))
     half = n_clus // 2
-    turns = [d for near in range(half) for d in (half + near, near + 1)][: n_clus - 1]
+    turns = list(range(1, n_clus))
+    sends = [d for near in range(half) for d in (near + 1, half + near)]
+    sends = [d for i, d in enumerate(sends) if d not in sends[:i]]
     for d in turns:
         label_copy[d].start()
     y_copy[0].start()
-    for d in turns:
+    for d in sends:
         row_copy[d].start()
     core_copy[0].start()
 
@@ -190,7 +194,7 @@
     for part in exact_parts(emb * 0.5):
         sums = sums + jnp.dot(members, part, preferred_element_type=jnp.float32)
     partial[...] = sums.reshape(n_src, n_clus * per, depth)
-    for e in range(1, n_src):
+    for e in range(2):
         partial_copy[e].start()
 
     def send_labels():
@@ -202,11 +206,15 @@
             shard_copy[e].start()
         return own_labels
 
+    def pair_sums():
+        for e in range(2):
+            partial_copy[e].wait_recv()
+        partial[2] = partial[2] + partial_in[1]
+        partial_copy[2].start()
+
     def reduce_sums():
-        total = partial[0]
-        for e in range(1, n_src):
-            partial_copy[e].wait_recv()
-            total = total + partial_in[e]
+        partial_copy[2].wait_recv()
+        total = partial[0] + partial_in[0] + partial_in[2]
         for d in range(n_clus):
             owned[d] = total[d * per : (d + 1) * per]
         for d in range(1, n_clus):
@@ -221,11 +229,16 @@
         for e in range(1, n_src):
             cent_copy[e].start()
 
-    def shard_maxima(e):
-        scores = dot_t(gathered[e].reshape(slots, depth), gathered[0].reshape(slots, depth))
+    def column_labels(e):
         other = jnp.transpose(jnp.broadcast_to(shard_labels[e], (128, slots)))
-        other = jnp.concatenate([other] * (slots // 128), axis=1)
-        allowed = other == own_labels
+        return jnp.concatenate([other] * (slots // 128), axis=1)
+
+    def shard_maxima(e, other, first=0, last=n_clus):
+        count = (last - first) * cap
+        scores = dot_t(
+            gathered[e, first:last].reshape(count, depth), gathered[0].reshape(slots, depth)
+        )
+        allowed = other[first * cap : last * cap] == own_labels
         if e == 0:
             allowed = allowed & (
                 lax.broadcasted_iota(jnp.int32, (slots, slots), 0)
@@ -243,26 +256,32 @@
         y_copy[d].start()
         core_copy[d].start()
         waiting.append(d)
+        if step == 0:
+            pair_sums()
         if step == 1:
             own_labels = send_labels()
-        if step == 2:
+        if step == 3:
             reduce_sums()
         if step >= 2:
             pass_on(waiting.pop(0))
     pass_on(waiting.pop(0))
-    best = shard_maxima(0)
+    best = shard_maxima(0, column_labels(0))
     for e in range(1, n_src):
         shard_copy[e].wait_recv()
     for d in range(n_clus):
         core_copy[d].wait_recv()
-    best = jnp.maximum(best, shard_maxima(1))
+    best = jnp.maximum(best, shard_maxima(1, column_labels(1)))
     for d in waiting:
         pass_on(d)
     finish_sums()
-    best = jnp.maximum(best, shard_maxima(2))
-    for d in range(n_clus):
+    best = jnp.maximum(best, shard_maxima(2, column_labels(2)))
+    other = column_labels(3)
+    for d in range(half):
         diag_copy[d].wait_recv()
-    maxima[0] = jnp.maximum(best, shard_maxima(3))
+    best = jnp.maximum(best, shard_maxima(3, other, 0, half))
+    for d in range(half, n_clus):
+        diag_copy[d].wait_recv()
+    maxima[0] = jnp.maximum(best, shard_maxima(3, other, half, n_clus))
     for d in turns:
         max_copy[d].start()
 
@@ -329,7 +348,7 @@
         ]
         + [pltpu.SemaphoreType.DMA((2,))],
         compiler_params=pltpu.CompilerParams(
-            collective_id=0, has_side_effects=True, vmem_limit_bytes=56 * 1024 * 1024
+            collective_id=0, has_side_effects=True, vmem_limit_bytes=55040 * 1024
         ),
         cost_estimate=pl.CostEstimate(
             flops=2 * slots * slots * n_src * depth, bytes_accessed=rows * depth * 4, transcendentals=0

time: 30.9 us -> 29.8 us (0.964)
  Pallas kernels: 28.2 us -> 27.2 us
    pallas_call x1, Pallas kernels: 28.2 us -> 27.2 us  [one_kernel(): pl.pallas_call(functools.partial(owner_kernel, n_clus, n_src, cap), out_s...]
where the time goes in v3:
time: 29.8 us; the launch traced here: 29.6 us
  Pallas kernels  27.2 us (91%)
  local copies, waits for them, and re-layouts  1.77 us (6%)
  between operations  0.65 us (2%)
    pallas_call x1, Pallas kernels, one_kernel(): pl.pallas_call(functools.partial(owner_kernel, n_clus, n_src, cap), out_s...  27.2 us
    unnamed x4, local copies, waits for them, and re-layouts  1.77 us

profile of v3, /device:TPU:0, one launch (start us, length us, event | category | flops | bytes accessed | tf_op | source)
XLA Modules:
  0.0 29.6 jit_solution(15107797656036080341)
XLA Ops:
  0.6 0.0 copy-start
  0.6 0.6 %copy-done = s32[128]{0:T(128)S(1)} copy-done((s32[128]{0:T(128)S(1)}, s32[128]{0:T(128)}, u32[]{:S(2)}) %copy-start) | copy-done | bytes 536
  1.3 27.2 %shard_map.41 = (f32[8,768]{1,0:T(8,128)S(1)}, f32[1,128]{1,0:T(1,128)S(1)}) custom-call(s32[1,128]{1,0:T(1,128)S(1)} %bitcast.2, f32[128,768]{1,0:T(8,128)} %emb_hbm.1), custom_call_target="tpu_custom_call" | custom-call | flops 402653184 | bytes 393216 | tf_op jit(solution)/shard_map/pallas_call | solution.py:323
  28.5 0.6 %copy.6 = f32[8,768]{1,0:T(8,128)} copy(f32[8,768]{1,0:T(8,128)S(1)} %get-tuple-element.8) | data formatting | bytes 49152
  29.1 0.5 %copy.7 = f32[128]{0:T(128)} copy(f32[128]{0:T(128)S(1)} %bitcast.3) | data formatting | bytes 1024
Async XLA Ops:
  0.6 0.7 %copy-start = (s32[128]{0:T(128)S(1)}, s32[128]{0:T(128)}, u32[]{:S(2)}) copy-start(s32[128]{0:T(128)} %param.3) | copy-start | bytes 1540

commit v4 on v3

--- a/solution.py
+++ b/solution.py
@@ -10,6 +10,7 @@
 CLUS_DEV = 8
 MESH = pl.DeviceIdType.MESH
 EPS = 1e-06
+LOADS = 4
 
 
 def partner(index, distance, count):
@@ -96,9 +97,16 @@
         )
 
     load_cluster = pltpu.make_async_copy(cluster_hbm, cluster_ref, load_sem.at[0])
-    load_rows = pltpu.make_async_copy(emb_hbm, emb_ref, load_sem.at[1])
+    band = rows // LOADS
+    load_rows = [
+        pltpu.make_async_copy(
+            emb_hbm.at[pl.ds(i * band, band)], emb_ref.at[pl.ds(i * band, band)], load_sem.at[1 + i]
+        )
+        for i in range(LOADS)
+    ]
     load_cluster.start()
-    load_rows.start()
+    for load in load_rows:
+        load.start()
     barrier = pltpu.get_barrier_semaphore()
     others = [at_clus[d] for d in range(1, n_clus)] + [at_src[e] for e in range(1, n_src)]
     for device in others:
@@ -123,9 +131,13 @@
         jnp.bfloat16
     )
 
-    load_rows.wait()
-    emb = emb_ref[...]
-    unit = (emb * lax.rsqrt(jnp.sum(emb * emb, axis=1, keepdims=True) + EPS)).astype(jnp.bfloat16)
+    units = []
+    for i, load in enumerate(load_rows):
+        load.wait()
+        part = emb_ref[i * band : (i + 1) * band]
+        norm = lax.rsqrt(jnp.sum(part * part, axis=1, keepdims=True) + EPS)
+        units.append((part * norm).astype(jnp.bfloat16))
+    unit = jnp.concatenate(units, axis=0)
     packed[...] = (
         jnp.dot(pick, unit, preferred_element_type=jnp.float32)
         .astype(jnp.bfloat16)
@@ -191,7 +203,7 @@
         lax.broadcasted_iota(jnp.int32, (count, rows), 0) == order, 2.0, 0.0
     ).astype(jnp.bfloat16)
     sums = jnp.zeros((count, depth), jnp.float32)
-    for part in exact_parts(emb * 0.5):
+    for part in exact_parts(emb_ref[...] * 0.5):
         sums = sums + jnp.dot(members, part, preferred_element_type=jnp.float32)
     partial[...] = sums.reshape(n_src, n_clus * per, depth)
     for e in range(2):
@@ -262,26 +274,29 @@
             own_labels = send_labels()
         if step == 3:
             reduce_sums()
-        if step >= 2:
+        if 2 <= step < len(turns) - 1:
             pass_on(waiting.pop(0))
-    pass_on(waiting.pop(0))
     best = shard_maxima(0, column_labels(0))
     for e in range(1, n_src):
         shard_copy[e].wait_recv()
     for d in range(n_clus):
         core_copy[d].wait_recv()
     best = jnp.maximum(best, shard_maxima(1, column_labels(1)))
+    last = waiting.pop()
     for d in waiting:
         pass_on(d)
     finish_sums()
-    best = jnp.maximum(best, shard_maxima(2, column_labels(2)))
-    other = column_labels(3)
+    over_y = column_labels(2)
+    best = jnp.maximum(best, shard_maxima(2, over_y, 0, half))
+    across = column_labels(3)
     for d in range(half):
         diag_copy[d].wait_recv()
-    best = jnp.maximum(best, shard_maxima(3, other, 0, half))
+    best = jnp.maximum(best, shard_maxima(3, across, 0, half))
+    pass_on(last)
+    best = jnp.maximum(best, shard_maxima(2, over_y, half, n_clus))
     for d in range(half, n_clus):
         diag_copy[d].wait_recv()
-    maxima[0] = jnp.maximum(best, shard_maxima(3, other, half, n_clus))
+    maxima[0] = jnp.maximum(best, shard_maxima(3, across, half, n_clus))
     for d in turns:
         max_copy[d].start()
 
@@ -346,14 +361,17 @@
             pltpu.SemaphoreType.DMA((2, count))
             for count in (n_clus, n_clus, n_clus, n_clus, n_clus, n_src, n_src, n_clus, n_src, n_clus)
         ]
-        + [pltpu.SemaphoreType.DMA((2,))],
+        + [pltpu.SemaphoreType.DMA((1 + LOADS,))],
         compiler_params=pltpu.CompilerParams(
-            collective_id=0, has_side_effects=True, vmem_limit_bytes=55040 * 1024
+            collective_id=0, has_side_effects=True, vmem_limit_bytes=32 * 1024 * 1024
         ),
         cost_estimate=pl.CostEstimate(
             flops=2 * slots * slots * n_src * depth, bytes_accessed=rows * depth * 4, transcendentals=0
         ),
-    )(cluster.reshape(1, rows), embeddings)
+    )(
+        pltpu.with_memory_space_constraint(cluster.reshape(1, rows), pltpu.HBM),
+        pltpu.with_memory_space_constraint(embeddings, pltpu.HBM),
+    )
     return centroids, nearest.reshape(rows)
 
 

time: 29.8 us -> 28.9 us (0.970)
  local copies, waits for them, and re-layouts: 1.77 us -> 1.12 us
  Pallas kernels: 27.2 us -> 26.9 us
    unnamed x4 -> x2, local copies, waits for them, and re-layouts: 1.77 us -> 1.12 us
where the time goes in v4:
time: 28.9 us; the launch traced here: 28.7 us
  Pallas kernels  26.9 us (93%)
  local copies, waits for them, and re-layouts  1.12 us (4%)
  between operations  0.64 us (2%)
    pallas_call x1, Pallas kernels, one_kernel(): pl.pallas_call(functools.partial(owner_kernel, n_clus, n_src, cap), out_s...  26.9 us
    unnamed x2, local copies, waits for them, and re-layouts  1.12 us

profile of v4, /device:TPU:0, one launch (start us, length us, event | category | flops | bytes accessed | tf_op | source)
XLA Modules:
  0.0 28.7 jit_solution(861541941136706199)
XLA Ops:
  0.6 26.9 %shard_map.41 = (f32[8,768]{1,0:T(8,128)S(1)}, f32[1,128]{1,0:T(1,128)S(1)}) custom-call(s32[1,128]{1,0:T(1,128)} %bitcast.3, f32[128,768]{1,0:T(8,128)} %emb_hbm.1), custom_call_target="tpu_custom_call" | custom-call | flops 402653184 | bytes 393216 | tf_op jit(solution)/shard_map/pallas_call | solution.py:338
  27.6 0.6 %copy.6 = f32[8,768]{1,0:T(8,128)} copy(f32[8,768]{1,0:T(8,128)S(1)} %get-tuple-element.8) | data formatting | bytes 49152
  28.2 0.5 %copy.7 = f32[128]{0:T(128)} copy(f32[128]{0:T(128)S(1)} %bitcast.2) | data formatting | bytes 1024

commit v5 on v4

--- a/solution.py
+++ b/solution.py
@@ -186,12 +186,12 @@
     pl.semaphore_wait(barrier, len(others))
     half = n_clus // 2
     turns = list(range(1, n_clus))
-    sends = [d for near in range(half) for d in (near + 1, half + near)]
-    sends = [d for i, d in enumerate(sends) if d not in sends[:i]]
+    follows = {turns[0]: half + 1}
+    follows.update({d: d + 2 for d in range(half, n_clus - 2)})
     for d in turns:
         label_copy[d].start()
     y_copy[0].start()
-    for d in sends:
+    for d in range(1, half + 1):
         row_copy[d].start()
     core_copy[0].start()
 
@@ -265,6 +265,8 @@
     waiting = [0]
     for step, d in enumerate(turns):
         row_copy[d].wait_recv()
+        if d in follows:
+            row_copy[follows[d]].start()
         y_copy[d].start()
         core_copy[d].start()
         waiting.append(d)

time: 28.9 us -> 31.6 us (1.093)
  Pallas kernels: 26.9 us -> 29.7 us
    pallas_call x1, Pallas kernels: 26.9 us -> 29.7 us  [one_kernel(): pl.pallas_call(functools.partial(owner_kernel, n_clus, n_src, cap), out_s...]
where the time goes in v5:
time: 31.6 us; the launch traced here: 31.4 us
  Pallas kernels  29.7 us (94%)
  local copies, waits for them, and re-layouts  1.12 us (4%)
  between operations  0.64 us (2%)
    pallas_call x1, Pallas kernels, one_kernel(): pl.pallas_call(functools.partial(owner_kernel, n_clus, n_src, cap), out_s...  29.7 us
    unnamed x2, local copies, waits for them, and re-layouts  1.12 us

profile of v5, /device:TPU:0, one launch (start us, length us, event | category | flops | bytes accessed | tf_op | source)
XLA Modules:
  0.0 31.4 jit_solution(3815931065855275010)
XLA Ops:
  0.6 29.7 %shard_map.41 = (f32[8,768]{1,0:T(8,128)S(1)}, f32[1,128]{1,0:T(1,128)S(1)}) custom-call(s32[1,128]{1,0:T(1,128)} %bitcast.3, f32[128,768]{1,0:T(8,128)} %emb_hbm.1), custom_call_target="tpu_custom_call" | custom-call | flops 402653184 | bytes 393216 | tf_op jit(solution)/shard_map/pallas_call | solution.py:340
  30.3 0.6 %copy.6 = f32[8,768]{1,0:T(8,128)} copy(f32[8,768]{1,0:T(8,128)S(1)} %get-tuple-element.8) | data formatting | bytes 49152
  30.9 0.5 %copy.7 = f32[128]{0:T(128)} copy(f32[128]{0:T(128)S(1)} %bitcast.2) | data formatting | bytes 1024

commit v6 on v4

--- a/solution.py
+++ b/solution.py
@@ -186,13 +186,13 @@
     pl.semaphore_wait(barrier, len(others))
     half = n_clus // 2
     turns = list(range(1, n_clus))
-    sends = [d for near in range(half) for d in (near + 1, half + near)]
-    sends = [d for i, d in enumerate(sends) if d not in sends[:i]]
+    sends = turns[half - 1 :] + turns[: half - 1]
+    for d in sends:
+        row_copy[d].start()
+        if d == turns[-1]:
+            y_copy[0].start()
     for d in turns:
         label_copy[d].start()
-    y_copy[0].start()
-    for d in sends:
-        row_copy[d].start()
     core_copy[0].start()
 
     order = (
@@ -272,7 +272,7 @@
             pair_sums()
         if step == 1:
             own_labels = send_labels()
-        if step == 3:
+        if step == 2:
             reduce_sums()
         if 2 <= step < len(turns) - 1:
             pass_on(waiting.pop(0))
@@ -300,6 +300,18 @@
     for d in turns:
         max_copy[d].start()
 
+    for copies in (
+        label_copy,
+        row_copy,
+        core_copy,
+        y_copy,
+        diag_copy,
+        partial_copy,
+        shard_copy,
+        owned_copy,
+    ):
+        for started in copies.values():
+            started.wait_send()
     for e in range(1, n_src):
         cent_copy[e].wait_recv()
     for shard in range(n_src):
@@ -311,20 +323,8 @@
         near = near + jnp.dot(part, pick, preferred_element_type=jnp.float32)
     near_ref[...] = near[:1]
 
-    for copies in (
-        label_copy,
-        row_copy,
-        core_copy,
-        y_copy,
-        diag_copy,
-        partial_copy,
-        shard_copy,
-        owned_copy,
-        cent_copy,
-        max_copy,
-    ):
-        for started in copies.values():
-            started.wait_send()
+    for started in list(cent_copy.values()) + list(max_copy.values()):
+        started.wait_send()
 
 
 def one_kernel(n_clus, n_src, embeddings, cluster):

time: 28.9 us -> 31.7 us (1.097)
  Pallas kernels: 26.9 us -> 29.8 us
    pallas_call x1, Pallas kernels: 26.9 us -> 29.8 us  [one_kernel(): pl.pallas_call(functools.partial(owner_kernel, n_clus, n_src, cap), out_s...]
where the time goes in v6:
time: 31.7 us; the launch traced here: 31.5 us
  Pallas kernels  29.8 us (94%)
  local copies, waits for them, and re-layouts  1.12 us (4%)
  between operations  0.64 us (2%)
    pallas_call x1, Pallas kernels, one_kernel(): pl.pallas_call(functools.partial(owner_kernel, n_clus, n_src, cap), out_s...  29.8 us
    unnamed x2, local copies, waits for them, and re-layouts  1.12 us

profile of v6, /device:TPU:0, one launch (start us, length us, event | category | flops | bytes accessed | tf_op | source)
XLA Modules:
  0.0 31.5 jit_solution(15601101739600395930)
XLA Ops:
  0.6 29.8 %shard_map.41 = (f32[8,768]{1,0:T(8,128)S(1)}, f32[1,128]{1,0:T(1,128)S(1)}) custom-call(s32[1,128]{1,0:T(1,128)} %bitcast.3, f32[128,768]{1,0:T(8,128)} %emb_hbm.1), custom_call_target="tpu_custom_call" | custom-call | flops 402653184 | bytes 393216 | tf_op jit(solution)/shard_map/pallas_call | solution.py:338
  30.4 0.6 %copy.6 = f32[8,768]{1,0:T(8,128)} copy(f32[8,768]{1,0:T(8,128)S(1)} %get-tuple-element.8) | data formatting | bytes 49152
  31.0 0.5 %copy.7 = f32[128]{0:T(128)} copy(f32[128]{0:T(128)S(1)} %bitcast.2) | data formatting | bytes 1024

commit v7 on v0

--- a/solution.py
+++ b/solution.py
@@ -1,9 +1,390 @@
+import functools
+
 import jax
 import jax.numpy as jnp
 from jax import lax
+from jax.experimental import pallas as pl
+from jax.experimental.pallas import tpu as pltpu
 from jax.sharding import PartitionSpec as P
 
 CLUS_DEV = 8
+MESH = pl.DeviceIdType.MESH
+EPS = 1e-06
+LOADS = 4
+
+
+def partner(index, distance, count):
+    total = 0
+    bit = 1
+    while bit < count:
+        value = (index // bit) % 2
+        total = total + bit * ((1 - value) if (distance // bit) % 2 else value)
+        bit *= 2
+    return total
+
+
+def exact_parts(values):
+    high = values.astype(jnp.bfloat16)
+    rest = values - high.astype(jnp.float32)
+    middle = rest.astype(jnp.bfloat16)
+    low = (rest - middle.astype(jnp.float32)).astype(jnp.bfloat16)
+    return high, middle, low
+
+
+def dot_t(left, right):
+    return lax.dot_general(left, right, (((1,), (1,)), ((), ())), preferred_element_type=jnp.float32)
+
+
+def xor(left, right, count):
+    total = 0
+    bit = 1
+    while bit < count:
+        a, b = (left // bit) % 2, (right // bit) % 2
+        total = total + bit * (a + b - 2 * a * b)
+        bit *= 2
+    return total
+
+
+def hub_kernel(
+    n_clus,
+    n_src,
+    cap,
+    cluster_hbm,
+    emb_hbm,
+    cent_ref,
+    near_ref,
+    cluster_ref,
+    emb_ref,
+    packed,
+    gathered,
+    label_out,
+    labels,
+    group_labels,
+    best,
+    maxima,
+    partial,
+    partial_in,
+    owned,
+    owned_in,
+    cents,
+    row_send,
+    row_recv,
+    label_send,
+    label_recv,
+    max_send,
+    max_recv,
+    partial_sem,
+    owned_sem,
+    cent_sem,
+    load_sem,
+):
+    rows, depth = emb_ref.shape
+    slots = n_clus * cap
+    per = CLUS_DEV // n_src
+    me = lax.axis_index("clus")
+    src = lax.axis_index("src")
+    plane, side, level = me // 2, me % 2, src // 2
+    is_hub = (src % 2 == 0) & (plane >= 1) & (plane <= 2)
+    my_owner = (plane - 1) * 4 + level * 2 + side
+    at_clus = [(partner(me, d, n_clus), src) for d in range(n_clus)]
+    at_src = [(me, partner(src, e, n_src)) for e in range(n_src)]
+    everyone = [
+        (d, e, (partner(me, d, n_clus), partner(src, e, n_src)))
+        for d in range(n_clus)
+        for e in range(n_src)
+    ]
+
+    def copy(source, target, send, recv, device):
+        return pltpu.make_async_remote_copy(
+            src_ref=source,
+            dst_ref=target,
+            send_sem=send,
+            recv_sem=recv,
+            device_id=device,
+            device_id_type=MESH,
+        )
+
+    def paired(source, target, sems, slot, device):
+        return copy(source, target, sems.at[0, slot], sems.at[1, slot], device)
+
+    band = rows // LOADS
+    load_rows = [
+        pltpu.make_async_copy(
+            emb_hbm.at[pl.ds(i * band, band)], emb_ref.at[pl.ds(i * band, band)], load_sem.at[1 + i]
+        )
+        for i in range(LOADS)
+    ]
+    load_cluster = pltpu.make_async_copy(cluster_hbm, cluster_ref, load_sem.at[0])
+    load_cluster.start()
+    for load in load_rows:
+        load.start()
+    barrier = pltpu.get_barrier_semaphore()
+    for _, _, device in everyone[1:]:
+        pl.semaphore_signal(barrier, inc=1, device_id=device, device_id_type=MESH)
+
+    load_cluster.wait()
+    cluster = cluster_ref[...]
+    within = cluster % CLUS_DEV
+    owner = cluster // CLUS_DEV
+    hits = lax.broadcasted_iota(jnp.int32, (n_clus, rows), 0) == owner
+    earlier = lax.broadcasted_iota(jnp.int32, (rows, rows), 0) < lax.broadcasted_iota(
+        jnp.int32, (rows, rows), 1
+    )
+    before = jnp.dot(
+        jnp.where(hits, 1.0, 0.0).astype(jnp.bfloat16),
+        jnp.where(earlier, 1.0, 0.0).astype(jnp.bfloat16),
+        preferred_element_type=jnp.float32,
+    )
+    place = jnp.sum(jnp.where(hits, before, 0.0), axis=0, keepdims=True).astype(jnp.int32)
+    slot_rows = lax.broadcasted_iota(jnp.int32, (slots, rows), 0)
+    pick = jnp.where(slot_rows == owner * cap + place, 1.0, 0.0).astype(jnp.bfloat16)
+    block = jnp.bitwise_xor(owner % 2, side) * n_src + jnp.bitwise_xor(
+        (owner // 2) % 2 * 2, src
+    )
+    spread = jnp.where(slot_rows == block * cap + place, 1.0, 0.0).astype(jnp.bfloat16)
+    marked = jnp.where(hits, (within + 1).astype(jnp.float32), 0.0).astype(jnp.bfloat16)
+    label_rows = dot_t(marked, spread)
+    for o in range(n_clus):
+        label_out[o] = label_rows[o : o + 1]
+
+    units = []
+    for i, load in enumerate(load_rows):
+        load.wait()
+        part = emb_ref[i * band : (i + 1) * band]
+        norm = lax.rsqrt(jnp.sum(part * part, axis=1, keepdims=True) + EPS)
+        units.append((part * norm).astype(jnp.bfloat16))
+    unit = jnp.concatenate(units, axis=0)
+    packed[...] = (
+        jnp.dot(pick, unit, preferred_element_type=jnp.float32)
+        .astype(jnp.bfloat16)
+        .reshape(n_clus, cap, depth)
+    )
+
+    near_plane = plane // 2
+    row_copy, label_copy, homes = [], [], []
+    for i in range(n_clus):
+        z = near_plane if i % 2 else 1 - near_plane
+        x = partner(side, (i // 2) % 2, 2)
+        y = partner(level, i // 4, 2)
+        o = z * 4 + y * 2 + x
+        device = ((1 + z) * 2 + x, 2 * y)
+        d, e = xor(me, device[0], n_clus), xor(src, device[1], n_src)
+        homes.append(o)
+        row_copy.append(
+            copy(packed.at[o], gathered.at[d, e], row_send.at[i], row_recv.at[d, e], device)
+        )
+        label_copy.append(
+            copy(label_out.at[o], labels.at[d, e], label_send.at[i], label_recv.at[d, e], device)
+        )
+    partial_copy = [
+        paired(partial.at[1], partial_in.at[0], partial_sem, 0, at_src[1]),
+        paired(partial.at[3], partial_in.at[1], partial_sem, 1, at_src[1]),
+        paired(partial.at[2], partial_in.at[2], partial_sem, 2, at_src[2]),
+    ]
+    owned_copy = {
+        d: paired(owned.at[d], owned_in.at[d], owned_sem, d, at_clus[d]) for d in range(1, n_clus)
+    }
+    cent_copy = {
+        e: paired(cents.at[0], cents.at[e], cent_sem, e, at_src[e]) for e in range(1, n_src)
+    }
+
+    pl.semaphore_wait(barrier, len(everyone) - 1)
+    for copies in (label_copy, row_copy):
+        for i in range(n_clus):
+            if i == 1:
+                @pl.when(jnp.logical_not(is_hub))
+                def _():
+                    copies[1].start()
+            else:
+                copies[i].start()
+
+    @pl.when(is_hub)
+    def _():
+        gathered[0, 0] = packed[homes[1]]
+        labels[0, 0] = label_out[homes[1]]
+
+    order = (
+        jnp.bitwise_xor(within // per, src) * (n_clus * per)
+        + jnp.bitwise_xor(owner, me) * per
+        + within % per
+    )
+    count = n_src * n_clus * per
+    members = jnp.where(
+        lax.broadcasted_iota(jnp.int32, (count, rows), 0) == order, 2.0, 0.0
+    ).astype(jnp.bfloat16)
+    sums = jnp.zeros((count, depth), jnp.float32)
+    for part in exact_parts(emb_ref[...] * 0.5):
+        sums = sums + jnp.dot(members, part, preferred_element_type=jnp.float32)
+    partial[...] = sums.reshape(n_src, n_clus * per, depth)
+    partial_copy[0].start()
+    partial_copy[1].start()
+    partial_copy[0].wait_recv()
+    partial_copy[1].wait_recv()
+    partial[2] = partial[2] + partial_in[1]
+    partial_copy[2].start()
+    partial_copy[2].wait_recv()
+    total = partial[0] + partial_in[0] + partial_in[2]
+    for d in range(n_clus):
+        owned[d] = total[d * per : (d + 1) * per]
+    for d in range(1, n_clus):
+        owned_copy[d].start()
+
+    def arrived(copy_source, target, sems, d, e):
+        copy(copy_source, target.at[d, e], sems.at[d, e], sems.at[d, e], at_src[1]).wait_recv()
+
+    def meet(group, earlier_groups):
+        width = 2 * n_src * cap
+        mine = jnp.zeros((1, width), jnp.float32)
+        for d in (2 * group, 2 * group + 1):
+            for e in range(n_src):
+                if d or e:
+                    arrived(label_out.at[0], labels, label_recv, d, e)
+                mine = mine + labels[d, e]
+        group_labels[group] = mine
+        column = jnp.transpose(jnp.broadcast_to(mine, (128, width)))
+        column = jnp.concatenate([column] * (width // 128), axis=1)
+        for d in (2 * group, 2 * group + 1):
+            for e in range(n_src):
+                if d or e:
+                    arrived(packed.at[0], gathered, row_recv, d, e)
+        left = gathered[2 * group : 2 * group + 2].reshape(width, depth)
+
+        def scores(other):
+            right = gathered[2 * other : 2 * other + 2].reshape(width, depth)
+            return dot_t(left, right), column == group_labels[other]
+
+        values, allowed = scores(group)
+        allowed = allowed & (
+            lax.broadcasted_iota(jnp.int32, (width, width), 0)
+            != lax.broadcasted_iota(jnp.int32, (width, width), 1)
+        )
+        top = jnp.max(jnp.where(allowed, values, -1.0), axis=0, keepdims=True)
+        across = None
+        for other in earlier_groups:
+            values, allowed = scores(other)
+            values = jnp.where(allowed, values, -1.0)
+            best[other] = jnp.maximum(best[other], jnp.max(values, axis=0, keepdims=True))
+            for j in range(width // 128):
+                piece = values[:, j * 128 : (j + 1) * 128]
+                across = piece if across is None else jnp.maximum(across, piece)
+        if across is not None:
+            top = jnp.maximum(top, jnp.max(jnp.transpose(across), axis=0, keepdims=True))
+        best[group] = top
+
+    @pl.when(is_hub)
+    def _():
+        meet(0, [])
+        meet(1, [0])
+
+    total = owned[0]
+    for d in range(1, n_clus):
+        owned_copy[d].wait_recv()
+        total = total + owned_in[d]
+    cents[0] = total * lax.rsqrt(jnp.sum(total * total, axis=1, keepdims=True) + EPS)
+    for e in range(1, n_src):
+        cent_copy[e].start()
+
+    def returned(d, e, device):
+        return copy(
+            best.at[d // 2],
+            maxima.at[my_owner],
+            max_send.at[d, e],
+            max_recv.at[my_owner],
+            device,
+        )
+
+    @pl.when(is_hub)
+    def _():
+        meet(3, [0, 1])
+        meet(2, [0, 1, 3])
+        for d, e, device in everyone[:0:-1]:
+            returned(d, e, device).start()
+        maxima[my_owner] = best[0]
+
+    for copies in (label_copy, row_copy):
+        for i in range(n_clus):
+            if i == 1:
+                @pl.when(jnp.logical_not(is_hub))
+                def _():
+                    copies[1].wait_send()
+            else:
+                copies[i].wait_send()
+    for started in partial_copy + list(owned_copy.values()) + list(cent_copy.values()):
+        started.wait_send()
+    for e in range(1, n_src):
+        cent_copy[e].wait_recv()
+    for shard in range(n_src):
+        cent_ref[shard * per : (shard + 1) * per, :] = cents[partner(src, shard, n_src)]
+
+    for o in range(n_clus):
+        @pl.when(jnp.logical_not(is_hub & (my_owner == o)))
+        def _():
+            copy(best.at[0], maxima.at[o], max_recv.at[o], max_recv.at[o], at_src[1]).wait_recv()
+    near = jnp.zeros((n_clus, rows), jnp.float32)
+    for part in exact_parts(jnp.concatenate([maxima[o] for o in range(n_clus)], axis=0)):
+        near = near + jnp.dot(part, spread, preferred_element_type=jnp.float32)
+    near_ref[...] = jnp.sum(jnp.where(hits, near, 0.0), axis=0, keepdims=True)
+
+    @pl.when(is_hub)
+    def _():
+        for d, e, device in everyone[1:]:
+            returned(d, e, device).wait_send()
+
+
+def one_kernel(n_clus, n_src, embeddings, cluster):
+    rows, depth = embeddings.shape
+    cap = 2 * rows // n_clus
+    slots = n_clus * cap
+    per = CLUS_DEV // n_src
+    f32, bf16 = jnp.float32, jnp.bfloat16
+    vmem = pl.BlockSpec(memory_space=pltpu.VMEM)
+    hbm = pl.BlockSpec(memory_space=pltpu.HBM)
+    dma = pltpu.SemaphoreType.DMA
+    centroids, nearest = pl.pallas_call(
+        functools.partial(hub_kernel, n_clus, n_src, cap),
+        out_shape=(
+            jax.ShapeDtypeStruct((CLUS_DEV, depth), f32),
+            jax.ShapeDtypeStruct((1, rows), f32),
+        ),
+        in_specs=[hbm, hbm],
+        out_specs=(vmem, vmem),
+        scratch_shapes=[
+            pltpu.VMEM((1, rows), jnp.int32),
+            pltpu.VMEM((rows, depth), f32),
+            pltpu.VMEM((n_clus, cap, depth), bf16),
+            pltpu.VMEM((n_clus, n_src, cap, depth), bf16),
+            pltpu.VMEM((n_clus, 1, slots), f32),
+            pltpu.VMEM((n_clus, n_src, 1, slots), f32),
+            pltpu.VMEM((n_clus // 2, 1, slots), f32),
+            pltpu.VMEM((n_clus // 2, 1, slots), f32),
+            pltpu.VMEM((n_clus, 1, slots), f32),
+            pltpu.VMEM((n_src, n_clus * per, depth), f32),
+            pltpu.VMEM((n_src, n_clus * per, depth), f32),
+            pltpu.VMEM((n_clus, per, depth), f32),
+            pltpu.VMEM((n_clus, per, depth), f32),
+            pltpu.VMEM((n_src, per, depth), f32),
+            dma((n_clus,)),
+            dma((n_clus, n_src)),
+            dma((n_clus,)),
+            dma((n_clus, n_src)),
+            dma((n_clus, n_src)),
+            dma((n_clus,)),
+            dma((2, n_src)),
+            dma((2, n_clus)),
+            dma((2, n_src)),
+            dma((1 + LOADS,)),
+        ],
+        compiler_params=pltpu.CompilerParams(
+            collective_id=0, has_side_effects=True, vmem_limit_bytes=32 * 1024 * 1024
+        ),
+        cost_estimate=pl.CostEstimate(
+            flops=2 * slots * slots * n_src * depth, bytes_accessed=rows * depth * 4, transcendentals=0
+        ),
+    )(
+        pltpu.with_memory_space_constraint(cluster.reshape(1, rows), pltpu.HBM),
+        pltpu.with_memory_space_constraint(embeddings, pltpu.HBM),
+    )
+    return centroids, nearest.reshape(rows)
 
 
 def block_maxima(current, own_unit, own_labels, own_global, other_unit, other_labels, other_global):
@@ -89,10 +470,21 @@
     return (centroids, nearest)
 
 
+def fits_one_kernel(n_clus, n_src, rows):
+    return n_clus == 8 and n_src == 4 and rows == 128
+
+
 def solution(mesh):
+    n_clus, n_src = mesh.shape["clus"], mesh.shape["src"]
+
+    def body(embeddings, cluster):
+        if fits_one_kernel(n_clus, n_src, embeddings.shape[0]):
+            return one_kernel(n_clus, n_src, embeddings, cluster)
+        return on_device(embeddings, cluster)
+
     placed = (P(("clus", "src"), None), P(("clus", "src")))
     return jax.shard_map(
-        on_device,
+        body,
         mesh=mesh,
         in_specs=placed,
         out_specs=(P("clus", None), P(("clus", "src"))),

time: 125 us -> 28.5 us (0.23)
  waiting for transfers between devices: 46.5 us -> 0 us
  Pallas kernels: 0 us -> 26.6 us
  blocking collectives: 20.9 us -> 0 us
  starting transfers between devices: 17.9 us -> 0 us
  between operations: 15.6 us -> 0.64 us
  other arithmetic: 9.22 us -> 0 us
  local copies, waits for them, and re-layouts: 8.74 us -> 1.12 us
  matrix products: 5.79 us -> 0 us
    reduce_scatter x1 -> x0, waiting for transfers between devices: 27 us -> none  [on_device(): lax.psum_scatter(jax.ops.segment_sum(embeddings, segment, num_segments=co...]
    pallas_call x0 -> x1, Pallas kernels: none -> 26.6 us  [one_kernel(): pl.pallas_call(functools.partial(hub_kernel, n_clus, n_src, cap), out_sha...]
    all_to_all x4 -> x0, waiting for transfers between devices: 19.4 us -> none  [the longest x1 8.97 us: on_device(): lax.all_to_all(send_unit, 'clus', split_axis=0, concat_axis=0, tiled=True)]
    all_to_all x4 -> x0, starting transfers between devices: 17.8 us -> none  [the longest x1 7.25 us: on_device(): lax.all_to_all(send_unit, 'clus', split_axis=0, concat_axis=0, tiled=True)]
    psum x1 -> x0, blocking collectives: 10.8 us -> none  [on_device(): owned = lax.psum(owned, 'src')]
    all_gather x2 -> x0, blocking collectives: 10.1 us -> none  [the longest x1 5.06 us: on_device(): piece_global = lax.all_gather(recv_global, 'src', axis=0, tiled=True)]
    dot_general x4 -> x0, matrix products: 5.79 us -> none  [block_maxima(): lax.dot_general(own_unit, other_unit, (((1,), (1,)), ((), ())), preferred...]
    all_to_all x8 -> x0, local copies, waits for them, and re-layouts: 3.28 us -> none  [the longest x3 1.26 us: on_device(): lax.all_to_all(send_labels, 'clus', split_axis=0, concat_axis=0, tiled=True)]
  transfers between devices with their start and end apart: 6 -> 0, of which waited for: 4 -> 0; matrix products, arithmetic and copies ran while one was open for 6% -> 0% of each run, Pallas kernels for 0% -> 0%
where the time goes in v7:
time: 28.5 us; the launch traced here: 28.3 us
  Pallas kernels  26.6 us (93%)
  local copies, waits for them, and re-layouts  1.12 us (4%)
  between operations  0.64 us (2%)
    pallas_call x1, Pallas kernels, one_kernel(): pl.pallas_call(functools.partial(hub_kernel, n_clus, n_src, cap), out_sha...  26.6 us
    unnamed x2, local copies, waits for them, and re-layouts  1.12 us

profile of v7, /device:TPU:0, one launch (start us, length us, event | category | flops | bytes accessed | tf_op | source)
XLA Modules:
  0.0 28.3 jit_solution(6056060809431508400)
XLA Ops:
  0.6 26.6 %shard_map.41 = (f32[8,768]{1,0:T(8,128)S(1)}, f32[1,128]{1,0:T(1,128)S(1)}) custom-call(s32[1,128]{1,0:T(1,128)} %bitcast.3, f32[128,768]{1,0:T(8,128)} %emb_hbm.1), custom_call_target="tpu_custom_call" | custom-call | flops 402653184 | bytes 393216 | tf_op jit(solution)/shard_map/pallas_call | solution.py:343
  27.2 0.6 %copy.6 = f32[8,768]{1,0:T(8,128)} copy(f32[8,768]{1,0:T(8,128)S(1)} %get-tuple-element.8) | data formatting | bytes 49152
  27.8 0.5 %copy.7 = f32[128]{0:T(128)} copy(f32[128]{0:T(128)S(1)} %bitcast.2) | data formatting | bytes 1024

commit v8 on v7

--- a/solution.py
+++ b/solution.py
@@ -60,6 +60,7 @@
     label_out,
     labels,
     group_labels,
+    columns,
     best,
     maxima,
     partial,
@@ -73,6 +74,8 @@
     label_recv,
     max_send,
     max_recv,
+    pass_sem,
+    pass_label_sem,
     partial_sem,
     owned_sem,
     cent_sem,
@@ -84,15 +87,18 @@
     me = lax.axis_index("clus")
     src = lax.axis_index("src")
     plane, side, level = me // 2, me % 2, src // 2
-    is_hub = (src % 2 == 0) & (plane >= 1) & (plane <= 2)
+    is_hub = (plane >= 1) & (plane <= 2)
     my_owner = (plane - 1) * 4 + level * 2 + side
     at_clus = [(partner(me, d, n_clus), src) for d in range(n_clus)]
     at_src = [(me, partner(src, e, n_src)) for e in range(n_src)]
-    everyone = [
-        (d, e, (partner(me, d, n_clus), partner(src, e, n_src)))
+    sides = n_src // 2
+    width = 2 * sides * cap
+    alike = [
+        (d, e, (partner(me, d, n_clus), partner(src, 2 * e, n_src)))
         for d in range(n_clus)
-        for e in range(n_src)
+        for e in range(sides)
     ]
+    arrival = [0, 1, 3, 2]
 
     def copy(source, target, send, recv, device):
         return pltpu.make_async_remote_copy(
@@ -119,7 +125,8 @@
     for load in load_rows:
         load.start()
     barrier = pltpu.get_barrier_semaphore()
-    for _, _, device in everyone[1:]:
+    reached = [device for _, _, device in alike[1:]] + [at_src[1], at_src[3]]
+    for device in reached:
         pl.semaphore_signal(barrier, inc=1, device_id=device, device_id_type=MESH)
 
     load_cluster.wait()
@@ -138,10 +145,8 @@
     place = jnp.sum(jnp.where(hits, before, 0.0), axis=0, keepdims=True).astype(jnp.int32)
     slot_rows = lax.broadcasted_iota(jnp.int32, (slots, rows), 0)
     pick = jnp.where(slot_rows == owner * cap + place, 1.0, 0.0).astype(jnp.bfloat16)
-    block = jnp.bitwise_xor(owner % 2, side) * n_src + jnp.bitwise_xor(
-        (owner // 2) % 2 * 2, src
-    )
-    spread = jnp.where(slot_rows == block * cap + place, 1.0, 0.0).astype(jnp.bfloat16)
+    block = jnp.bitwise_xor(owner % 2, side) * sides + jnp.bitwise_xor((owner // 2) % 2, level)
+    spread = jnp.where(slot_rows[:width] == block * cap + place, 1.0, 0.0).astype(jnp.bfloat16)
     marked = jnp.where(hits, (within + 1).astype(jnp.float32), 0.0).astype(jnp.bfloat16)
     label_rows = dot_t(marked, spread)
     for o in range(n_clus):
@@ -167,11 +172,14 @@
         x = partner(side, (i // 2) % 2, 2)
         y = partner(level, i // 4, 2)
         o = z * 4 + y * 2 + x
-        device = ((1 + z) * 2 + x, 2 * y)
-        d, e = xor(me, device[0], n_clus), xor(src, device[1], n_src)
+        device = ((1 + z) * 2 + x, 2 * y + src % 2)
+        near = xor(me, device[0], n_clus)
+        e = i // 4
+        far = near // 2
+        d = (far + far // 2 - 2 * (far // 3)) * 2 + near % 2
         homes.append(o)
         row_copy.append(
-            copy(packed.at[o], gathered.at[d, e], row_send.at[i], row_recv.at[d, e], device)
+            copy(packed.at[o], gathered.at[0, d, e], row_send.at[i], row_recv.at[d, e], device)
         )
         label_copy.append(
             copy(label_out.at[o], labels.at[d, e], label_send.at[i], label_recv.at[d, e], device)
@@ -188,7 +196,7 @@
         e: paired(cents.at[0], cents.at[e], cent_sem, e, at_src[e]) for e in range(1, n_src)
     }
 
-    pl.semaphore_wait(barrier, len(everyone) - 1)
+    pl.semaphore_wait(barrier, len(reached))
     for copies in (label_copy, row_copy):
         for i in range(n_clus):
             if i == 1:
@@ -200,7 +208,7 @@
 
     @pl.when(is_hub)
     def _():
-        gathered[0, 0] = packed[homes[1]]
+        gathered[0, 0, 0] = packed[homes[1]]
         labels[0, 0] = label_out[homes[1]]
 
     order = (
@@ -229,52 +237,71 @@
     for d in range(1, n_clus):
         owned_copy[d].start()
 
-    def arrived(copy_source, target, sems, d, e):
-        copy(copy_source, target.at[d, e], sems.at[d, e], sems.at[d, e], at_src[1]).wait_recv()
-
-    def meet(group, earlier_groups):
-        width = 2 * n_src * cap
+    def arrived(copy_source, target, sem):
+        copy(copy_source, target, sem, sem, at_src[1]).wait_recv()
+
+    def pass_rows(g):
+        pair = pl.ds(2 * g, 2)
+        return paired(gathered.at[0, pair], gathered.at[1, pair], pass_sem, g, at_src[1])
+
+    def pass_labels(g):
+        return paired(group_labels.at[0, g], group_labels.at[1, g], pass_label_sem, g, at_src[1])
+
+    def rows_of(core, first, last):
+        held = gathered[core, 2 * first : 2 * last]
+        return held.reshape((last - first) * width, depth)
+
+    def label_row(core, last):
+        return jnp.concatenate([group_labels[core, g] for g in range(last)], axis=1)
+
+    def column_of(row):
+        return jnp.transpose(jnp.broadcast_to(row, (width, width)))
+
+    def raise_best(values, first):
+        top = jnp.max(values, axis=0, keepdims=True)
+        for j in range(top.shape[1] // width):
+            best[first + j] = jnp.maximum(best[first + j], top[:, j * width : (j + 1) * width])
+
+    def meet(g):
+        blocks = [(d, e) for d in (2 * g, 2 * g + 1) for e in range(sides)]
         mine = jnp.zeros((1, width), jnp.float32)
-        for d in (2 * group, 2 * group + 1):
-            for e in range(n_src):
-                if d or e:
-                    arrived(label_out.at[0], labels, label_recv, d, e)
-                mine = mine + labels[d, e]
-        group_labels[group] = mine
-        column = jnp.transpose(jnp.broadcast_to(mine, (128, width)))
-        column = jnp.concatenate([column] * (width // 128), axis=1)
-        for d in (2 * group, 2 * group + 1):
-            for e in range(n_src):
-                if d or e:
-                    arrived(packed.at[0], gathered, row_recv, d, e)
-        left = gathered[2 * group : 2 * group + 2].reshape(width, depth)
-
-        def scores(other):
-            right = gathered[2 * other : 2 * other + 2].reshape(width, depth)
-            return dot_t(left, right), column == group_labels[other]
-
-        values, allowed = scores(group)
-        allowed = allowed & (
-            lax.broadcasted_iota(jnp.int32, (width, width), 0)
-            != lax.broadcasted_iota(jnp.int32, (width, width), 1)
-        )
-        top = jnp.max(jnp.where(allowed, values, -1.0), axis=0, keepdims=True)
-        across = None
-        for other in earlier_groups:
-            values, allowed = scores(other)
-            values = jnp.where(allowed, values, -1.0)
-            best[other] = jnp.maximum(best[other], jnp.max(values, axis=0, keepdims=True))
-            for j in range(width // 128):
-                piece = values[:, j * 128 : (j + 1) * 128]
-                across = piece if across is None else jnp.maximum(across, piece)
-        if across is not None:
-            top = jnp.maximum(top, jnp.max(jnp.transpose(across), axis=0, keepdims=True))
-        best[group] = top
+        for d, e in blocks:
+            if d or e:
+                arrived(label_out.at[0], labels.at[d, e], label_recv.at[d, e])
+            mine = mine + labels[d, e]
+        group_labels[0, g] = mine
+        pass_labels(g).start()
+        best[g] = jnp.full((1, width), -1.0, jnp.float32)
+        for d, e in blocks:
+            if d or e:
+                arrived(packed.at[0], gathered.at[0, d, e], row_recv.at[d, e])
+        pass_rows(g).start()
+        own_labels = label_row(0, g + 1)
+        wide = (width, (g + 1) * width)
+        row_place = lax.broadcasted_iota(jnp.int32, wide, 0) + g * width
+        allowed = jnp.concatenate([column_of(mine)] * (g + 1), axis=1) == own_labels
+        allowed = allowed & (row_place != lax.broadcasted_iota(jnp.int32, wide, 1))
+        values = jnp.where(allowed, dot_t(rows_of(0, g, g + 1), rows_of(0, 0, g + 1)), -1.0)
+        raise_best(values, 0)
+        if g:
+            across = values[:, :width]
+            for j in range(1, g):
+                across = jnp.maximum(across, values[:, j * width : (j + 1) * width])
+            raise_best(jnp.transpose(across), g)
+            earlier_rows = jnp.concatenate([columns[j] for j in range(g)], axis=0)
+            values = dot_t(rows_of(1, 0, g), rows_of(0, g, g + 1))
+            raise_best(jnp.where(earlier_rows == mine, values, -1.0), g)
+        pass_labels(g).wait_recv()
+        columns[g] = column_of(group_labels[1, g])
+        allowed = jnp.concatenate([columns[g]] * (g + 1), axis=1) == own_labels
+        pass_rows(g).wait_recv()
+        values = dot_t(rows_of(1, g, g + 1), rows_of(0, 0, g + 1))
+        raise_best(jnp.where(allowed, values, -1.0), 0)
 
     @pl.when(is_hub)
     def _():
-        meet(0, [])
-        meet(1, [0])
+        meet(0)
+        meet(1)
 
     total = owned[0]
     for d in range(1, n_clus):
@@ -286,7 +313,7 @@
 
     def returned(d, e, device):
         return copy(
-            best.at[d // 2],
+            best.at[arrival[d // 2]],
             maxima.at[my_owner],
             max_send.at[d, e],
             max_recv.at[my_owner],
@@ -295,9 +322,9 @@
 
     @pl.when(is_hub)
     def _():
-        meet(3, [0, 1])
-        meet(2, [0, 1, 3])
-        for d, e, device in everyone[:0:-1]:
+        meet(2)
+        meet(3)
+        for d, e, device in alike[:0:-1]:
             returned(d, e, device).start()
         maxima[my_owner] = best[0]
 
@@ -327,8 +354,11 @@
 
     @pl.when(is_hub)
     def _():
-        for d, e, device in everyone[1:]:
+        for d, e, device in alike[1:]:
             returned(d, e, device).wait_send()
+        for g in range(len(arrival)):
+            pass_rows(g).wait_send()
+            pass_labels(g).wait_send()
 
 
 def one_kernel(n_clus, n_src, embeddings, cluster):
@@ -336,6 +366,8 @@
     cap = 2 * rows // n_clus
     slots = n_clus * cap
     per = CLUS_DEV // n_src
+    sides, levels = n_src // 2, n_clus // 2
+    width = 2 * sides * cap
     f32, bf16 = jnp.float32, jnp.bfloat16
     vmem = pl.BlockSpec(memory_space=pltpu.VMEM)
     hbm = pl.BlockSpec(memory_space=pltpu.HBM)
@@ -352,23 +384,26 @@
             pltpu.VMEM((1, rows), jnp.int32),
             pltpu.VMEM((rows, depth), f32),
             pltpu.VMEM((n_clus, cap, depth), bf16),
-            pltpu.VMEM((n_clus, n_src, cap, depth), bf16),
-            pltpu.VMEM((n_clus, 1, slots), f32),
-            pltpu.VMEM((n_clus, n_src, 1, slots), f32),
-            pltpu.VMEM((n_clus // 2, 1, slots), f32),
-            pltpu.VMEM((n_clus // 2, 1, slots), f32),
-            pltpu.VMEM((n_clus, 1, slots), f32),
+            pltpu.VMEM((2, n_clus, sides, cap, depth), bf16),
+            pltpu.VMEM((n_clus, 1, width), f32),
+            pltpu.VMEM((n_clus, sides, 1, width), f32),
+            pltpu.VMEM((2, levels, 1, width), f32),
+            pltpu.VMEM((levels, width, width), f32),
+            pltpu.VMEM((levels, 1, width), f32),
+            pltpu.VMEM((n_clus, 1, width), f32),
             pltpu.VMEM((n_src, n_clus * per, depth), f32),
             pltpu.VMEM((n_src, n_clus * per, depth), f32),
             pltpu.VMEM((n_clus, per, depth), f32),
             pltpu.VMEM((n_clus, per, depth), f32),
             pltpu.VMEM((n_src, per, depth), f32),
             dma((n_clus,)),
-            dma((n_clus, n_src)),
+            dma((n_clus, sides)),
             dma((n_clus,)),
-            dma((n_clus, n_src)),
-            dma((n_clus, n_src)),
+            dma((n_clus, sides)),
+            dma((n_clus, sides)),
             dma((n_clus,)),
+            dma((2, levels)),
+            dma((2, levels)),
             dma((2, n_src)),
             dma((2, n_clus)),
             dma((2, n_src)),

time: 28.5 us -> 29.7 us (1.042)
  Pallas kernels: 26.6 us -> 27.8 us
    pallas_call x1, Pallas kernels: 26.6 us -> 27.8 us  [one_kernel(): pl.pallas_call(functools.partial(hub_kernel, n_clus, n_src, cap), out_sha...]
where the time goes in v8:
time: 29.7 us; the launch traced here: 29.6 us
  Pallas kernels  27.8 us (94%)
  local copies, waits for them, and re-layouts  1.12 us (4%)
  between operations  0.64 us (2%)
    pallas_call x1, Pallas kernels, one_kernel(): pl.pallas_call(functools.partial(hub_kernel, n_clus, n_src, cap), out_sha...  27.8 us
    unnamed x2, local copies, waits for them, and re-layouts  1.12 us

profile of v8, /device:TPU:0, one launch (start us, length us, event | category | flops | bytes accessed | tf_op | source)
XLA Modules:
  0.0 29.6 jit_solution(15259530227195051619)
XLA Ops:
  0.6 27.8 %shard_map.41 = (f32[8,768]{1,0:T(8,128)S(1)}, f32[1,128]{1,0:T(1,128)S(1)}) custom-call(s32[1,128]{1,0:T(1,128)} %bitcast.3, f32[128,768]{1,0:T(8,128)} %emb_hbm.1), custom_call_target="tpu_custom_call" | custom-call | flops 402653184 | bytes 393216 | tf_op jit(solution)/shard_map/pallas_call | solution.py:375
  28.4 0.6 %copy.6 = f32[8,768]{1,0:T(8,128)} copy(f32[8,768]{1,0:T(8,128)S(1)} %get-tuple-element.8) | data formatting | bytes 49152
  29.0 0.5 %copy.7 = f32[128]{0:T(128)} copy(f32[128]{0:T(128)S(1)} %bitcast.2) | data formatting | bytes 1024

commit v9 on v7

--- a/solution.py
+++ b/solution.py
@@ -189,14 +189,17 @@
     }
 
     pl.semaphore_wait(barrier, len(everyone) - 1)
-    for copies in (label_copy, row_copy):
-        for i in range(n_clus):
+    def send(copies, places):
+        for i in places:
             if i == 1:
                 @pl.when(jnp.logical_not(is_hub))
                 def _():
                     copies[1].start()
             else:
                 copies[i].start()
+
+    send(label_copy, range(n_clus))
+    send(row_copy, range(4))
 
     @pl.when(is_hub)
     def _():
@@ -218,10 +221,12 @@
     partial[...] = sums.reshape(n_src, n_clus * per, depth)
     partial_copy[0].start()
     partial_copy[1].start()
+    send(row_copy, range(4, 6))
     partial_copy[0].wait_recv()
     partial_copy[1].wait_recv()
     partial[2] = partial[2] + partial_in[1]
     partial_copy[2].start()
+    send(row_copy, range(6, n_clus))
     partial_copy[2].wait_recv()
     total = partial[0] + partial_in[0] + partial_in[2]
     for d in range(n_clus):
@@ -276,6 +281,23 @@
         meet(0, [])
         meet(1, [0])
 
+    def returned(d, e, device):
+        return copy(
+            best.at[d // 2],
+            maxima.at[my_owner],
+            max_send.at[d, e],
+            max_recv.at[my_owner],
+            device,
+        )
+
+    @pl.when(is_hub)
+    def _():
+        meet(3, [0, 1])
+        meet(2, [0, 1, 3])
+        for d, e, device in everyone[:0:-1]:
+            returned(d, e, device).start()
+        maxima[my_owner] = best[0]
+
     total = owned[0]
     for d in range(1, n_clus):
         owned_copy[d].wait_recv()
@@ -283,23 +305,6 @@
     cents[0] = total * lax.rsqrt(jnp.sum(total * total, axis=1, keepdims=True) + EPS)
     for e in range(1, n_src):
         cent_copy[e].start()
-
-    def returned(d, e, device):
-        return copy(
-            best.at[d // 2],
-            maxima.at[my_owner],
-            max_send.at[d, e],
-            max_recv.at[my_owner],
-            device,
-        )
-
-    @pl.when(is_hub)
-    def _():
-        meet(3, [0, 1])
-        meet(2, [0, 1, 3])
-        for d, e, device in everyone[:0:-1]:
-            returned(d, e, device).start()
-        maxima[my_owner] = best[0]
 
     for copies in (label_copy, row_copy):
         for i in range(n_clus):

time: 28.5 us -> 28.7 us (level)
  no operation moved by 1% of the time
where the time goes in v9:
time: 28.7 us; the launch traced here: 28.5 us
  Pallas kernels  26.7 us (93%)
  local copies, waits for them, and re-layouts  1.12 us (4%)
  between operations  0.64 us (2%)
    pallas_call x1, Pallas kernels, one_kernel(): pl.pallas_call(functools.partial(hub_kernel, n_clus, n_src, cap), out_sha...  26.7 us
    unnamed x2, local copies, waits for them, and re-layouts  1.12 us

profile of v9, /device:TPU:0, one launch (start us, length us, event | category | flops | bytes accessed | tf_op | source)
XLA Modules:
  0.0 28.5 jit_solution(12699065384573616752)
XLA Ops:
  0.6 26.7 %shard_map.41 = (f32[8,768]{1,0:T(8,128)S(1)}, f32[1,128]{1,0:T(1,128)S(1)}) custom-call(s32[1,128]{1,0:T(1,128)} %bitcast.3, f32[128,768]{1,0:T(8,128)} %emb_hbm.1), custom_call_target="tpu_custom_call" | custom-call | flops 402653184 | bytes 393216 | tf_op jit(solution)/shard_map/pallas_call | solution.py:348
  27.4 0.6 %copy.6 = f32[8,768]{1,0:T(8,128)} copy(f32[8,768]{1,0:T(8,128)S(1)} %get-tuple-element.8) | data formatting | bytes 49152
  28.0 0.5 %copy.7 = f32[128]{0:T(128)} copy(f32[128]{0:T(128)S(1)} %bitcast.2) | data formatting | bytes 1024

commit v10 on v7

--- a/solution.py
+++ b/solution.py
@@ -329,6 +329,17 @@
     def _():
         for d, e, device in everyone[1:]:
             returned(d, e, device).wait_send()
+
+
+def store_kernel(cent_ref, near_ref, cent_hbm, near_hbm, sem):
+    stores = [
+        pltpu.make_async_copy(cent_ref, cent_hbm, sem.at[0]),
+        pltpu.make_async_copy(near_ref, near_hbm, sem.at[1]),
+    ]
+    for store in stores:
+        store.start()
+    for store in stores:
+        store.wait()
 
 
 def one_kernel(n_clus, n_src, embeddings, cluster):
@@ -384,6 +395,16 @@
         pltpu.with_memory_space_constraint(cluster.reshape(1, rows), pltpu.HBM),
         pltpu.with_memory_space_constraint(embeddings, pltpu.HBM),
     )
+    centroids, nearest = pl.pallas_call(
+        store_kernel,
+        out_shape=(
+            jax.ShapeDtypeStruct((CLUS_DEV, depth), f32),
+            jax.ShapeDtypeStruct((1, rows), f32),
+        ),
+        in_specs=[vmem, vmem],
+        out_specs=(hbm, hbm),
+        scratch_shapes=[dma((2,))],
+    )(centroids, nearest)
     return centroids, nearest.reshape(rows)
 
 

time: 28.5 us -> 29.9 us (1.049)
  Pallas kernels: 26.6 us -> 28 us
    pallas_call x0 -> x1, Pallas kernels: none -> 1.36 us  [one_kernel(): pl.pallas_call(store_kernel, out_shape=(jax.ShapeDtypeStruct((CLUS_DEV, d...]
    unnamed x2 -> x4, local copies, waits for them, and re-layouts: 1.12 us -> 1.09 us
where the time goes in v10:
time: 29.9 us; the launch traced here: 29.7 us
  Pallas kernels  28 us (94%)
  local copies, waits for them, and re-layouts  1.09 us (4%)
  between operations  0.65 us (2%)
    pallas_call x1, Pallas kernels, one_kernel(): pl.pallas_call(functools.partial(hub_kernel, n_clus, n_src, cap), out_sha...  26.6 us
    pallas_call x1, Pallas kernels, one_kernel(): pl.pallas_call(store_kernel, out_shape=(jax.ShapeDtypeStruct((CLUS_DEV, d...  1.36 us
    unnamed x4, local copies, waits for them, and re-layouts  1.09 us

profile of v10, /device:TPU:0, one launch (start us, length us, event | category | flops | bytes accessed | tf_op | source)
XLA Modules:
  0.0 29.7 jit_solution(17572689356449685824)
XLA Ops:
  0.6 26.6 %shard_map.41 = (f32[8,768]{1,0:T(8,128)S(1)}, f32[1,128]{1,0:T(1,128)S(1)}) custom-call(s32[1,128]{1,0:T(1,128)} %bitcast.2, f32[128,768]{1,0:T(8,128)} %emb_hbm.1), custom_call_target="tpu_custom_call" | custom-call | flops 402653184 | bytes 393216 | tf_op jit(solution)/shard_map/pallas_call | solution.py:354
  27.2 0.0 copy-start
  27.2 0.6 %copy-done = f32[8,768]{1,0:T(8,128)} copy-done((f32[8,768]{1,0:T(8,128)}, f32[8,768]{1,0:T(8,128)S(1)}, u32[]{:S(2)}) %copy-start) | copy-done | bytes 24600
  27.8 0.0 copy-start.1
  27.8 0.5 %copy-done.1 = f32[1,128]{1,0:T(1,128)} copy-done((f32[1,128]{1,0:T(1,128)}, f32[1,128]{1,0:T(1,128)S(1)}, u32[]{:S(2)}) %copy-start.1) | copy-done | bytes 536
  28.3 1.4 %shard_map.42 = (f32[8,768]{1,0:T(8,128)}, f32[1,128]{1,0:T(1,128)}) custom-call(f32[8,768]{1,0:T(8,128)} %copy-done, f32[1,128]{1,0:T(1,128)} %copy-done.1), custom_call_target="tpu_custom_call" | custom-call | tf_op jit(solution)/shard_map/pallas_call | solution.py:398
Async XLA Ops:
  27.2 0.6 %copy-start = (f32[8,768]{1,0:T(8,128)}, f32[8,768]{1,0:T(8,128)S(1)}, u32[]{:S(2)}) copy-start(f32[8,768]{1,0:T(8,128)S(1)} %get-tuple-element.6.cent_ref) | copy-start | bytes 73732
  27.8 0.5 %copy-start.1 = (f32[1,128]{1,0:T(1,128)}, f32[1,128]{1,0:T(1,128)S(1)}, u32[]{:S(2)}) copy-start(f32[1,128]{1,0:T(1,128)S(1)} %get-tuple-element.7.near_ref) | copy-start | bytes 1540
